TPU v7x, 256 devices: a whole 4x4x8 slice. The times are simulated.
256 devices in a mesh: users: 16 (over y_hi, z), score: 16 (over y_lo, x, core).
Axes of the slice: x: 4, y: 4 (y_hi: 2, y_lo: 2; y = y_hi * 2 + y_lo), z: 8, core: 2. Of those that a mesh axis runs over, the one named last changes fastest.
Arguments:
- candidates: bfloat16 [32, 6144, 1024], P('users', 'score'), may hold values from -6 to 6
- history: bfloat16 [32, 512, 1024], P('users', 'score'), may hold values from -6 to 6
- proj_weight: bfloat16 [1024, 4, 1024], P(('users', 'score')), may hold values from -0.1875 to 0.1875
- out_weight: bfloat16 [1024, 1024], replicated, may hold values from -0.1875 to 0.1875
- hist_len: int32 [32], P('users'), may hold values from 1 to 512, as said below
- cand_count: int32 [32], P('users'), may hold values from 1 to 6144, as said below
Outputs:
- scored: bfloat16 [32, 6144, 1024], P('users', 'score')
Inputs may be any that keep to these rules, and one draw needn't show every extreme that they name: `hist_len`: some user has exactly 512 live events. `cand_count`: some user has exactly 6144 live candidates.
All inputs are finite; a program needn't handle non-finite values.
Results may differ from a plain program's by a relative error of at most 0.0051.
Values may be sent and summed in bfloat16 or wider, within the bound.
A program may use at most 128 MiB of HBM per device.

v0:
```python
import math

import jax
import jax.numpy as jnp
from jax import lax
from jax.sharding import PartitionSpec as P

HEADS = 8


def body(candidates, history, proj_weight, out_weight, hist_len, cand_count):
    users_here, cand_rows, model_width = candidates.shape
    head_count = HEADS
    head_size = model_width // head_count
    score_scale = 1.0 / math.sqrt(head_size)
    cand_flat = candidates.reshape(-1, model_width)
    hist_flat = history.reshape(-1, model_width)
    whole_weight = lax.all_gather(proj_weight, ("users", "score"), axis=0, tiled=True)
    all_rows = whole_weight.reshape(-1, model_width)
    pair_rows = whole_weight[:, 0:2, :].reshape(-1, model_width)
    cand_part = jax.nn.silu(
        jnp.einsum("rd,kd->rk", cand_flat, all_rows, preferred_element_type=jnp.float32)
    ).astype(jnp.bfloat16)
    hist_part = jax.nn.silu(
        jnp.einsum("rd,kd->rk", hist_flat, pair_rows, preferred_element_type=jnp.float32)
    ).astype(jnp.bfloat16)
    cand_parts = jnp.transpose(
        cand_part.reshape(users_here, cand_rows, model_width, 4), (0, 1, 3, 2)
    )
    hist_parts = jnp.transpose(hist_part.reshape(users_here, -1, model_width, 2), (0, 1, 3, 2))
    head_shape = (users_here, cand_rows, head_count, head_size)
    own_key = cand_parts[:, :, 0].reshape(head_shape)
    own_value = cand_parts[:, :, 1].reshape(head_shape)
    queries = cand_parts[:, :, 2].reshape(head_shape)
    user_gate = cand_parts[:, :, 3]
    hist_keys = hist_parts[:, :, 0]
    hist_values = hist_parts[:, :, 1]
    longest = jnp.max(hist_len)
    zero_acc = jnp.zeros(head_shape, jnp.float32)
    key_piece = lax.all_gather(hist_keys, "score", axis=1, tiled=True)
    value_piece = lax.all_gather(hist_values, "score", axis=1, tiled=True)
    key_count = key_piece.shape[1]

    def compute(current):
        key_heads = key_piece.reshape(users_here, key_count, head_count, head_size)
        value_heads = value_piece.reshape(users_here, key_count, head_count, head_size)
        scores = (
            jnp.einsum("uchd,ujhd->uhcj", queries, key_heads, preferred_element_type=jnp.float32)
            * score_scale
        )
        positions = jnp.arange(key_count, dtype=jnp.int32)
        is_live = positions[None, :] < hist_len[:, None]
        weights = jnp.where(is_live[:, None, None, :], jax.nn.silu(scores), 0.0).astype(
            jnp.bfloat16
        )
        return jnp.einsum(
            "uhcj,ujhd->uchd", weights, value_heads, preferred_element_type=jnp.float32
        )

    def keep(current):
        return current

    attended = lax.cond(jnp.int32(0) < longest, compute, keep, zero_acc)
    self_weight = jax.nn.silu(
        jnp.einsum("uchd,uchd->uch", queries, own_key, preferred_element_type=jnp.float32)
        * score_scale
    )
    attended = attended + self_weight[..., None] * own_value.astype(jnp.float32)
    attn_rows = attended.reshape(users_here, cand_rows, model_width)
    row_mean = jnp.mean(attn_rows, axis=2, keepdims=True)
    centered = attn_rows - row_mean
    row_var = jnp.mean(centered * centered, axis=2, keepdims=True)
    normed = centered * lax.rsqrt(row_var + 1e-06)
    gated_rows = (normed * user_gate.astype(jnp.float32)).astype(jnp.bfloat16)
    mixed_rows = jnp.dot(
        gated_rows.reshape(-1, model_width), out_weight, preferred_element_type=jnp.float32
    )
    mixed_rows = mixed_rows.reshape(users_here, cand_rows, model_width) + candidates.astype(
        jnp.float32
    )
    slot_index = lax.axis_index("score") * cand_rows + jnp.arange(cand_rows, dtype=jnp.int32)
    cand_live = slot_index[None, :] < cand_count[:, None]
    return jnp.where(cand_live[:, :, None], mixed_rows, 0.0).astype(jnp.bfloat16)


def solution(mesh):
    in_specs = (
        P("users", "score", None),
        P("users", "score", None),
        P(("users", "score"), None, None),
        P(),
        P("users"),
        P("users"),
    )
    out_specs = P("users", "score", None)
    return jax.shard_map(body, mesh=mesh, in_specs=in_specs, out_specs=out_specs, check_vma=False)
```

profile of v0, /device:TPU:1, one launch (start us, length us, event | category | flops | bytes accessed | tf_op | source)
XLA Modules:
  0.0 588.7 jit_solution(9199112340249090701)
XLA Ops:
  6.5 0.0 copy-start
  6.5 0.0 all-gather.6.cloned.1.call-start
  6.5 0.7 all-gather.6.cloned.1.call-update
  7.3 0.0 all-gather.10.cloned.1.call-start
  7.3 424.5 %all-gather.6.cloned.1.call-done = bf16[1024,4,1024]{2,1,0:T(4,128)(2,1)} async-done(((bf16[4,4,1024]{2,1,0:T(4,128)(2,1)}), bf16[1024,4,1024]{2,1,0:T(4,128)(2,1)}) %all-gather.6.cloned.1.call-update) | async-done | bytes 8388624 | tf_op jit(solution)/shard_map/all_gather | solution.py:18
  431.8 8.2 %slice.28 = bf16[1024,2,1024]{2,1,0:T(2,128)(2,1)} slice(bf16[1024,4,1024]{2,1,0:T(4,128)(2,1)} %all-gather.6.cloned.1.call-done), slice={[0:1024], [0:2], [0:1024]} | slice | bytes 8388608 | tf_op jit(solution)/shard_map/slice | solution.py:20
  440.0 0.0 copy-start.4
  440.0 7.2 %reshape.115 = bf16[2048,1024]{1,0:T(8,128)(2,1)} reshape(bf16[1024,2,1024]{2,1,0:T(2,128)(2,1)} %slice.28) | data formatting | bytes 8388608 | tf_op jit(solution)/shard_map/reshape | solution.py:20
  447.3 0.0 copy-done.4
  447.3 3.6 multiply_convert_fusion.1
  450.9 0.0 copy-start.2
  450.9 0.0 copy-start.3
  450.9 1.0 copy.39
  451.9 2.4 reshape.116
  454.4 1.7 fusion.26
  456.1 2.0 copy.44
  458.1 0.0 all-gather.10.cloned.1.call-update
  458.1 0.2 all-gather.8.cloned.1.call-start
  458.3 2.0 copy.40
  460.3 0.0 all-gather.8.cloned.1.call-update
  460.4 0.0 copy-done.2
  460.4 0.6 reduce_max.9
  461.7 0.0 copy-done.3
  461.7 0.1 broadcast_compare_fusion
  461.8 12.5 %reshape.118 = bf16[4096,1024]{1,0:T(8,128)(2,1)} reshape(bf16[1024,4,1024]{2,1,0:T(4,128)(2,1)} %all-gather.6.cloned.1.call-done) | data formatting | bytes 16777216 | tf_op jit(solution)/shard_map/reshape | solution.py:19
  474.3 12.6 %multiply_convert_fusion = bf16[768,4096]{1,0:T(8,128)(2,1)} fusion(bf16[768,1024]{1,0:T(8,128)(2,1)} %bitcast.56, bf16[4096,1024]{1,0:T(8,128)(2,1)} %reshape.118), kind=kOutput, calls=%fused_computation.10 | convolution fusion | flops 6458179584 | bytes 16252928 | tf_op jit(solution)/shard_map/rd,kd->rk/dot_general | solution.py:22
  486.9 8.6 %copy.41 = bf16[768,4096]{0,1:T(8,128)(2,1)} copy(bf16[768,4096]{1,0:T(8,128)(2,1)} %multiply_convert_fusion) | data formatting | bytes 12582912 | tf_op jit(solution)/shard_map/convert_element_type | solution.py:23
  495.5 12.8 %reshape.119 = bf16[2,384,1024,4]{1,0,3,2:T(2,128)(2,1)} reshape(bf16[768,4096]{0,1:T(8,128)(2,1)} %copy.41) | data formatting | bytes 12582912 | tf_op jit(solution)/shard_map/reshape | solution.py:28
  508.3 16.3 %copy.42 = bf16[2,384,1024,4]{2,1,3,0:T(8,128)(2,1)} copy(bf16[2,384,1024,4]{1,0,3,2:T(2,128)(2,1)} %reshape.119) | data formatting | bytes 12582912 | tf_op jit(solution)/shard_map/reshape | solution.py:28
  524.6 5.3 fusion.25
  529.9 1.6 copy.61
  531.5 2.6 copy.43
  534.1 3.2 copy.55
  537.3 3.3 multiply_reduce_fusion
  540.5 0.1 copy.56
  540.7 3.6 copy.48
  544.3 0.0 all-gather.10.cloned.1.call-done
  544.3 0.0 all-gather.8.cloned.1.call-done
  544.4 19.3 %conditional.1 = (f32[2,384,8,128]{3,1,2,0:T(8,128)}) conditional(s32[]{:T(128)} %convert_element_type.37, () %tuple.11, (s32[2]{0:T(128)S(1)}, bf16[2,512,1024]{2,0,1:T(2,128)(2,1)}, bf16[2,384,8,128]{1,3,2,0:T(8,128)(2,1)}, bf16[2,512,1024]{2,0,1:T(2,128)(2,1)}) %tuple.31), branch_computations={%region_1.2_spmd, %region_2.3_spmd} | conditional | flops 1632633856 | bytes 17303568 | solution.py:63
  544.6 4.4 reshape.130
  549.0 0.1 iota_compare_fusion
  549.0 4.4 reshape.129
  553.4 10.2 %fusion.6 = f32[2,384,8,128]{3,1,2,0:T(8,128)} fusion(bf16[2,512,8,128]{3,2,0,1:T(8,128)(2,1)} %reshape.130, pred[2,512]{1,0:T(4,128)(4,1)S(1)} %iota_compare_fusion, bf16[2,384,8,128]{1,3,2,0:T(8,128)(2,1)} %get-tuple-element.30, bf16[2,512,8,128]{3,2,0,1:T(8,128)(2,1)} %reshape.129), kind=kOutput, calls=%fused_computation.5 | convolution fusion | flops 1632632832 | bytes 8913920 | tf_op jit(solution)/shard_map/cond/branch_1_fun/uhcj,ujhd->uchd/dot_general | solution.py:56
  563.6 3.5 copy.49
  567.2 3.5 fusion.24
  570.7 0.0 copy-start.1
  570.7 1.6 copy-done.1
  572.3 0.3 multiply_reduce_fusion.1
  572.7 3.6 copy.50
  576.3 0.0 copy-done
  576.3 5.9 select_convert_fusion.4
  (4 shorter events, 0.0 us)
Async XLA Ops:
  6.5 569.7 %copy-start = (bf16[1024,1024]{1,0:T(8,128)(2,1)S(1)}, bf16[1024,1024]{1,0:T(8,128)(2,1)}, u32[]{:S(2)}) copy-start(bf16[1024,1024]{1,0:T(8,128)(2,1)} %param.11) | copy-start | bytes 6291460
  6.5 425.3 %all-gather.6.cloned.1.call-start = ((), (), s32[]{:S(2)}) async-start(), calls=%async_computation | async-start | bytes 8421376 | tf_op jit(solution)/shard_map/all_gather | solution.py:18
  7.3 537.1 %all-gather.10.cloned.1.call-start = ((), (), s32[]{:S(2)}) async-start(), calls=%async_computation.2 | async-start | bytes 2228224 | tf_op jit(solution)/shard_map/all_gather | solution.py:41
  440.0 7.2 %copy-start.4 = (bf16[2,32,1024]{2,1,0:T(8,128)(2,1)S(1)}, bf16[2,32,1024]{2,1,0:T(8,128)(2,1)}, u32[]{:S(2)}) copy-start(bf16[2,32,1024]{2,1,0:T(8,128)(2,1)} %param.9) | copy-start | bytes 393220
  450.9 9.5 %copy-start.2 = (s32[2]{0:T(128)S(1)}, s32[2]{0:T(128)}, u32[]{:S(2)}) copy-start(s32[2]{0:T(128)} %param.12) | copy-start | bytes 28
  450.9 10.8 %copy-start.3 = (s32[2]{0:T(128)S(1)}, s32[2]{0:T(128)}, u32[]{:S(2)}) copy-start(s32[2]{0:T(128)} %param.13) | copy-start | bytes 28
  458.1 86.2 %all-gather.8.cloned.1.call-start = ((), (), s32[]{:S(2)}) async-start(), calls=%async_computation.1 | async-start | bytes 2228224 | tf_op jit(solution)/shard_map/all_gather | solution.py:40
  570.7 1.7 copy-start.1
Sparse Core Ops, SparseCore 0:
  9.2 422.5 all-gather.5
  458.2 35.0 all-gather.9
  495.2 36.6 all-gather.7
where the time goes:
time: 591 us; the launch traced here: 589 us
  waiting for transfers between devices  425 us (72%)
  local copies, waits for them, and re-layouts  103 us (17%)
  matrix products  32.3 us (5%)
  between operations  13.9 us (2%)
  other arithmetic  13.2 us (2%)
    all_gather x1, waiting for transfers between devices, body(): lax.all_gather(proj_weight, ('users', 'score'), axis=0, tiled=True)  425 us
    reshape x2, local copies, waits for them, and re-layouts, body(): cand_part.reshape(users_here, cand_rows, model_width, 4)  29 us
    dot_general x1, matrix products, body(): jnp.einsum('rd,kd->rk', cand_flat, all_rows, preferred_element_type=jnp.f...  12.6 us
    reshape x1, local copies, waits for them, and re-layouts, body(): all_rows = whole_weight.reshape(-1, model_width)  12.5 us
  transfers between devices with their start and end apart: 3, of which 1 were waited for; matrix products, arithmetic and copies ran while one was open for 14% of the time, Pallas kernels for 0%

commit v1 on v0

v1 whole, which is shorter than its diff:
```python
import math

import jax
import jax.numpy as jnp
from jax import lax
from jax.experimental import pallas as pl
from jax.experimental.pallas import tpu as pltpu
from jax.sharding import PartitionSpec as P

MESH = pl.DeviceIdType.MESH
HEADS = 8
NX, NY, NZ = 4, 4, 8
BF16, F32 = jnp.bfloat16, jnp.float32
COLS_X, COLS_Y, COLS_Z = pl.ds(0, 256), pl.ds(256, 384), pl.ds(640, 384)
NSEM = 160


def nt_dot(a, b):
    return lax.dot_general(a, b, (((1,), (1,)), ((), ())), preferred_element_type=F32)


def half_silu(t):
    return t + t * jnp.tanh(t)


def kernel(
    cand_ref, hist_ref, proj_ref, ow_ref, hlen_ref, ccount_ref, out_ref,
    G, H, T, R, cand_v, ow_v, mask_v, attn, gate, gated, out_v, send_sem, recv_sem, local_sem,
):
    u = lax.axis_index("users")
    s = lax.axis_index("score")
    z = lax.rem(u, NZ)
    yhi = lax.div(u, NZ)
    c = lax.rem(s, 2)
    x = lax.rem(lax.div(s, 2), NX)
    ylo = lax.div(s, 8)
    y = yhi * 2 + ylo
    oc = 1 - c

    def dev(px, py, pz, pc):
        return (lax.div(py, 2) * NZ + pz, lax.rem(py, 2) * 8 + px * 2 + pc)

    def up(pos, n, k):
        return lax.rem(pos + k + n, n)

    xo = x + 1 - 2 * lax.rem(x, 2)
    yo = y + 1 - 2 * ylo
    right = {"x": dev(up(x, NX, 1), y, z, c), "y": dev(x, up(y, NY, 1), z, c), "z": dev(x, y, up(z, NZ, 1), c)}
    left = {"x": dev(up(x, NX, -1), y, z, c), "y": dev(x, up(y, NY, -1), z, c), "z": dev(x, y, up(z, NZ, -1), c)}
    sib = dev(x, y, z, oc)
    diag = dev(xo, y, z, oc)

    local = [
        pltpu.make_async_copy(hist_ref, H.at[c, x, ylo], local_sem.at[0]),
        pltpu.make_async_copy(cand_ref, cand_v, local_sem.at[1]),
        pltpu.make_async_copy(ow_ref, ow_v, local_sem.at[2]),
    ]
    for copy in local:
        copy.start()

    barrier = pltpu.get_barrier_semaphore()
    partners = [right["x"], left["x"], right["y"], left["y"], right["z"], left["z"], sib, diag]
    for partner in partners:
        pl.semaphore_signal(barrier, inc=1, device_id=partner, device_id_type=MESH)

    row16 = lax.broadcasted_iota(jnp.int32, (16, 1024), 0)
    for p in range(4):
        tile = jnp.zeros((16, 1024), F32)
        for f in range(4):
            row = proj_ref[f].astype(F32)[p : p + 1]
            tile = jnp.where(row16 == f, jnp.broadcast_to(row, (16, 1024)), tile)
        T[p] = tile.astype(BF16)

    pl.semaphore_wait(barrier, len(partners))

    state = {"k": 0}
    sent = []

    def new_sem():
        k = state["k"]
        state["k"] = k + 1
        return k

    def rcopy(src, dst, k, target):
        return pltpu.make_async_remote_copy(
            src_ref=src, dst_ref=dst, send_sem=send_sem.at[k], recv_sem=recv_sem.at[k],
            device_id=target, device_id_type=MESH,
        )

    def send(src, dst, k, target):
        copy = rcopy(src, dst, k, target)
        copy.start()
        sent.append(copy)

    def wait(dst, k):
        rcopy(dst, dst, k, sib).wait_recv()

    p0 = lax.rem(x, 2) * 2 + c
    xbase = lax.div(x, 2) * 2
    exchange = []
    for step in (1, 2, 3):
        q = lax.rem(p0 + step, 4)
        k = new_sem()
        send(T.at[q], R.at[p0], k, dev(xbase + lax.div(q, 2), y, z, lax.rem(q, 2)))
        exchange.append((k, lax.rem(p0 - step + 4, 4)))
    R[p0] = T[p0]

    k_hist_y = new_sem()
    send(hist_ref, H.at[c, x, ylo], k_hist_y, dev(x, yo, z, c))

    for k, src in exchange:
        wait(R.at[src], k)
    rows = lax.broadcasted_iota(jnp.int32, (16, 64), 0)
    cols = lax.broadcasted_iota(jnp.int32, (16, 64), 1)
    pick = (cols == (rows - (rows & 3)) * 4 + (rows & 3)).astype(F32).astype(BF16)
    received = R[...].reshape(64, 1024)
    slab = lax.dot_general(pick, received, (((1,), (0,)), ((), ())), preferred_element_type=F32)
    G[c, x, y, z] = slab.astype(BF16)

    pos = {"x": x, "y": y, "z": z}
    size = {"x": NX, "y": NY, "z": NZ}
    whole = slice(None)

    def ring(stages, pending):
        for number, (axis, block) in enumerate(stages):
            last = number == len(stages) - 1
            r, n = pos[axis], size[axis]

            def share(at, half):
                if last:
                    k = new_sem()
                    send(block(c, at, half), block(c, at, half), k, sib)
                    pending.append((block(oc, at, half), k))

            got = []
            for j in range(n // 2):
                for at, half, k in got:
                    wait(block(c, at, half), k)
                ends = j == n // 2 - 1
                ahead = []
                for sign, target, half in ((1, right[axis], 0), (-1, left[axis], 1)):
                    half = half if ends else None
                    if ends and half == 1 and block(c, r, 1) is None:
                        continue
                    k = new_sem()
                    mine = up(r, n, -sign * j)
                    send(block(c, mine, half), block(c, mine, half), k, target)
                    ahead.append((up(r, n, -sign * (j + 1)), half, k))
                if j == 0:
                    share(r, None)
                for at, half, k in got:
                    share(at, half)
                got = ahead
                yield
            for at, half, k in got:
                wait(block(c, at, half), k)
                share(at, half)

    def halves(half, n):
        return whole if half is None else pl.ds(half * (n // 2), n // 2)

    def z_first(columns):
        def block(plane, at, half):
            return None if half == 1 else G.at[plane, x, y, at, :, columns]
        return ("z", block)

    color_x = [
        z_first(COLS_X),
        ("y", lambda p, at, h: G.at[p, x, at, halves(h, NZ), :, COLS_X]),
        ("x", lambda p, at, h: G.at[p, at, halves(h, NY), :, :, COLS_X]),
    ]
    color_y = [
        z_first(COLS_Y),
        ("x", lambda p, at, h: G.at[p, at, y, halves(h, NZ), :, COLS_Y]),
        ("y", lambda p, at, h: G.at[p, halves(h, NX), at, :, :, COLS_Y]),
    ]
    color_z = [
        ("x", lambda p, at, h: None if h == 1 else G.at[p, at, y, z, :, COLS_Z]),
        ("y", lambda p, at, h: G.at[p, halves(h, NX), at, z, :, COLS_Z]),
        ("z", lambda p, at, h: G.at[p, halves(h, NX), :, at, :, COLS_Z]),
    ]
    pending = []
    local[0].wait()
    rings = [ring(color_z, pending), ring(color_x, pending), ring(color_y, pending)]
    for run in rings:
        next(run)
    wait(H.at[c, x, 1 - ylo], k_hist_y)
    hist_ring = ring([("x", lambda p, at, h: H.at[p, at] if h is None else H.at[p, at, h])], pending)
    rings.append(hist_ring)
    next(hist_ring)
    for _ in range(12):
        for run in list(rings):
            try:
                next(run)
            except StopIteration:
                rings.remove(run)
    assert not rings
    local[1].wait()
    local[2].wait()
    for view, k in pending:
        wait(view, k)

    head_size = 128
    score_half = 0.5 / math.sqrt(head_size)
    users_here = cand_v.shape[0]

    q = lax.broadcasted_iota(jnp.int32, (512, 128), 0)
    event = (((q >> 5) & 1) * 8 + ((q >> 6) & 3) * 2 + (q >> 8)) * 32 + (q & 31)
    for user in range(users_here):
        mask_v[user] = (event < hlen_ref[user]).astype(F32)

    def head_weight(hi, zp, a, plane):
        return jnp.concatenate(
            [
                G[plane, a + 2 * xp, hi * 2 + yl, pl.ds(2 * zp, 2)].reshape(32, 1024)
                for xp in range(2)
                for yl in range(2)
            ],
            axis=0,
        )

    def one_head(h, carry):
        hi, zp = lax.div(h, 4), lax.rem(h, 4)
        w_kv = jnp.concatenate([head_weight(hi, zp, 0, 0), head_weight(hi, zp, 0, 1)], axis=0)
        w_qg = jnp.concatenate([head_weight(hi, zp, 1, 0), head_weight(hi, zp, 1, 1)], axis=0)
        at = pl.ds(pl.multiple_of(h * 128, 128), 128)
        for user in range(users_here):
            rows_c = cand_v[user]
            rows_h = H[:, :, :, user].reshape(512, 1024)
            kv_h = half_silu(0.5 * nt_dot(rows_h, w_kv))
            keys = kv_h[:, :128].astype(BF16)
            values = (kv_h[:, 128:] * mask_v[user]).astype(BF16)
            qg = half_silu(0.5 * nt_dot(rows_c, w_qg)).astype(BF16)
            kv_c = half_silu(0.5 * nt_dot(rows_c, w_kv)).astype(BF16)
            queries = qg[:, :128]
            gate[user, :, at] = qg[:, 128:]
            weights = half_silu(nt_dot(queries, keys) * score_half).astype(BF16)
            att = lax.dot_general(weights, values, (((1,), (0,)), ((), ())), preferred_element_type=F32)
            own = jnp.sum(queries.astype(F32) * kv_c[:, :128].astype(F32), axis=1, keepdims=True)
            own = half_silu(own * score_half)
            attn[user, :, at] = att + own * kv_c[:, 128:].astype(F32)
        return carry

    lax.fori_loop(0, HEADS, one_head, 0)

    def ow_rows():
        parts = []
        for h in range(HEADS):
            for xp in range(2):
                for yl in range(2):
                    for zl in range(2):
                        first = h * 128 + zl * 64 + yl * 32 + xp * 16
                        parts.append((first, 16))
        return parts

    order = ow_rows()
    slot0 = s * 384
    for user in range(users_here):
        def norm(i, carry):
            block = pl.ds(pl.multiple_of(i * 64, 64), 64)
            rows_a = attn[user, block]
            mean = jnp.sum(rows_a, axis=1, keepdims=True) * (1.0 / 1024)
            centered = rows_a - mean
            var = jnp.sum(centered * centered, axis=1, keepdims=True) * (1.0 / 1024)
            normed = centered * lax.rsqrt(var + 1e-06)
            gated[user, block] = (normed * gate[user, block].astype(F32)).astype(BF16)
            return carry

        lax.fori_loop(0, 6, norm, 0)
        for n in range(4):
            ncols = pl.ds(n * 256, 256)
            ow = jnp.concatenate([ow_v[first : first + size_, n * 256 : n * 256 + 256] for first, size_ in order], axis=0)
            mixed = jnp.dot(gated[user], ow, preferred_element_type=F32)
            mixed = mixed + cand_v[user, :, ncols].astype(F32)
            slot = slot0 + lax.broadcasted_iota(jnp.int32, (384, 256), 0)
            out_v[user, :, ncols] = jnp.where(slot < ccount_ref[user], mixed, 0.0).astype(BF16)
        pltpu.make_async_copy(out_v.at[user], out_ref.at[user], local_sem.at[3 + user]).start()
    for user in range(users_here):
        pltpu.make_async_copy(out_v.at[user], out_ref.at[user], local_sem.at[3 + user]).wait()
    for copy in sent:
        copy.wait_send()
    assert state["k"] <= NSEM


def body(candidates, history, proj_weight, out_weight, hist_len, cand_count):
    anyspace = pl.BlockSpec(memory_space=pl.ANY)
    smem = pl.BlockSpec(memory_space=pltpu.SMEM)
    vmem = pl.BlockSpec(memory_space=pltpu.VMEM)
    return pl.pallas_call(
        kernel,
        out_shape=jax.ShapeDtypeStruct(candidates.shape, BF16),
        in_specs=[anyspace, anyspace, vmem, anyspace, smem, smem],
        out_specs=anyspace,
        scratch_shapes=[
            pltpu.VMEM((2, NX, NY, NZ, 16, 1024), BF16),
            pltpu.VMEM((2, NX, 2, 2, 32, 1024), BF16),
            pltpu.VMEM((4, 16, 1024), BF16),
            pltpu.VMEM((4, 16, 1024), BF16),
            pltpu.VMEM((2, 384, 1024), BF16),
            pltpu.VMEM((1024, 1024), BF16),
            pltpu.VMEM((2, 512, 128), F32),
            pltpu.VMEM((2, 384, 1024), F32),
            pltpu.VMEM((2, 384, 1024), BF16),
            pltpu.VMEM((2, 384, 1024), BF16),
            pltpu.VMEM((2, 384, 1024), BF16),
            pltpu.SemaphoreType.DMA((NSEM,)),
            pltpu.SemaphoreType.DMA((NSEM,)),
            pltpu.SemaphoreType.DMA((5,)),
        ],
        compiler_params=pltpu.CompilerParams(
            collective_id=0, has_side_effects=True, vmem_limit_bytes=56 * 1024 * 1024
        ),
    )(candidates, history, proj_weight, out_weight, hist_len, cand_count)


def solution(mesh):
    in_specs = (
        P("users", "score", None),
        P("users", "score", None),
        P(("users", "score"), None, None),
        P(),
        P("users"),
        P("users"),
    )
    out_specs = P("users", "score", None)
    return jax.shard_map(body, mesh=mesh, in_specs=in_specs, out_specs=out_specs, check_vma=False)
```

time: 591 us -> 88.7 us (0.15)
  waiting for transfers between devices: 425 us -> 0 us
  local copies, waits for them, and re-layouts: 103 us -> 2.67 us
  Pallas kernels: 0 us -> 85.9 us
  matrix products: 32.3 us -> 0 us
  between operations: 13.9 us -> 0.01 us
  other arithmetic: 13.2 us -> 0 us
    all_gather x3 -> x0, waiting for transfers between devices: 425 us -> none  [the longest x1 425 us: body(): lax.all_gather(proj_weight, ('users', 'score'), axis=0, tiled=True)]
    pallas_call x0 -> x1, Pallas kernels: none -> 85.9 us  [body(): pl.pallas_call(kernel, out_shape=jax.ShapeDtypeStruct(candidates.shape, B...]
    reshape x8 -> x0, local copies, waits for them, and re-layouts: 63.6 us -> none  [the longest x2 29 us: body(): cand_part.reshape(users_here, cand_rows, model_width, 4)]
    dot_general x4 -> x0, matrix products: 32.3 us -> none  [the longest x1 12.6 us: body(): jnp.einsum('rd,kd->rk', cand_flat, all_rows, preferred_element_type=jnp.f...]
    slice x5 -> x0, local copies, waits for them, and re-layouts: 16.5 us -> none  [the longest x1 8.22 us: body(): pair_rows = whole_weight[:, 0:2, :].reshape(-1, model_width)]
    convert_element_type x3 -> x0, local copies, waits for them, and re-layouts: 13.2 us -> none  [the longest x1 8.63 us: body(): cand_part = jax.nn.silu(jnp.einsum('rd,kd->rk', cand_flat, all_rows, pref...]
  transfers between devices with their start and end apart: 3 -> 0, of which waited for: 1 -> 0; matrix products, arithmetic and copies ran while one was open for 14% -> 0% of each run, Pallas kernels for 0% -> 0%
where the time goes in v1:
time: 88.7 us; the launch traced here: 88.6 us
  Pallas kernels  85.9 us (97%)
  local copies, waits for them, and re-layouts  2.67 us (3%)
    pallas_call x1, Pallas kernels, body(): pl.pallas_call(kernel, out_shape=jax.ShapeDtypeStruct(candidates.shape, B...  85.9 us
    unnamed x1, local copies, waits for them, and re-layouts  2.67 us

profile of v1, /device:TPU:1, one launch (start us, length us, event | category | flops | bytes accessed | tf_op | source)
XLA Modules:
  0.0 88.6 jit_solution(5121871328945880784)
XLA Ops:
  0.0 85.9 %shard_map.64 = bf16[2,384,1024]{2,1,0:T(8,128)(2,1)} custom-call(bf16[2,384,1024]{2,1,0:T(8,128)(2,1)} %cand_ref.1, bf16[2,32,1024]{2,1,0:T(8,128)(2,1)} %hist_ref.1, bf16[4,4,1024]{2,1,0:T(4,128)(2,1)} %proj_ref.1, bf16[1024,1024]{1,0:T(8,128)(2,1)} %ow_ref.1, s32[2]{0:T(128)} %hlen_ref.1, s32[2]{0:T(128)} %ccount_ref.1), custom_call_target="tpu_custom_call" | custom-call | tf_op jit(solution)/shard_map/pallas_call | solution.py:289
  85.9 2.7 %copy.8 = bf16[2,384,1024]{2,1,0:T(8,128)(2,1)} copy(bf16[2,384,1024]{2,1,0:T(8,128)(2,1)} %shard_map.64) | data formatting | bytes 3145728

commit v2 on v1

--- a/solution.py
+++ b/solution.py
@@ -1,3 +1,4 @@
+import functools
 import math
 
 import jax
@@ -12,7 +13,9 @@
 NX, NY, NZ = 4, 4, 8
 BF16, F32 = jnp.bfloat16, jnp.float32
 COLS_X, COLS_Y, COLS_Z = pl.ds(0, 256), pl.ds(256, 384), pl.ds(640, 384)
-NSEM = 160
+COLS_XY = pl.ds(0, 640)
+SLOT = {0: 0, -1: 1, 1: 2, -2: 3, 2: 4, -3: 5, 3: 6, 4: 7, -4: 7}
+NSEM = 128
 
 
 def nt_dot(a, b):
@@ -45,8 +48,6 @@
 
     xo = x + 1 - 2 * lax.rem(x, 2)
     yo = y + 1 - 2 * ylo
-    right = {"x": dev(up(x, NX, 1), y, z, c), "y": dev(x, up(y, NY, 1), z, c), "z": dev(x, y, up(z, NZ, 1), c)}
-    left = {"x": dev(up(x, NX, -1), y, z, c), "y": dev(x, up(y, NY, -1), z, c), "z": dev(x, y, up(z, NZ, -1), c)}
     sib = dev(x, y, z, oc)
     diag = dev(xo, y, z, oc)
 
@@ -59,7 +60,8 @@
         copy.start()
 
     barrier = pltpu.get_barrier_semaphore()
-    partners = [right["x"], left["x"], right["y"], left["y"], right["z"], left["z"], sib, diag]
+    partners = [dev(up(x, NX, k), y, z, c) for k in (1, 3, 2)] + [dev(x, up(y, NY, k), z, c) for k in (1, 3, 2)]
+    partners += [dev(x, y, up(z, NZ, k), c) for k in (1, 7, 2, 6, 3, 5, 4)] + [sib, diag]
     for partner in partners:
         pl.semaphore_signal(barrier, inc=1, device_id=partner, device_id_type=MESH)
 
@@ -83,14 +85,13 @@
 
     def rcopy(src, dst, k, target):
         return pltpu.make_async_remote_copy(
-            src_ref=src, dst_ref=dst, send_sem=send_sem.at[k], recv_sem=recv_sem.at[k],
+            src_ref=src(), dst_ref=dst(), send_sem=send_sem.at[k], recv_sem=recv_sem.at[k],
             device_id=target, device_id_type=MESH,
         )
 
     def send(src, dst, k, target):
-        copy = rcopy(src, dst, k, target)
-        copy.start()
-        sent.append(copy)
+        rcopy(src, dst, k, target).start()
+        sent.append((src, k))
 
     def wait(dst, k):
         rcopy(dst, dst, k, sib).wait_recv()
@@ -101,104 +102,123 @@
     for step in (1, 2, 3):
         q = lax.rem(p0 + step, 4)
         k = new_sem()
-        send(T.at[q], R.at[p0], k, dev(xbase + lax.div(q, 2), y, z, lax.rem(q, 2)))
+        send(functools.partial(T.at.__getitem__, q), lambda: R.at[p0], k, dev(xbase + lax.div(q, 2), y, z, lax.rem(q, 2)))
         exchange.append((k, lax.rem(p0 - step + 4, 4)))
     R[p0] = T[p0]
 
     k_hist_y = new_sem()
-    send(hist_ref, H.at[c, x, ylo], k_hist_y, dev(x, yo, z, c))
+    send(lambda: hist_ref, lambda: H.at[c, x, ylo], k_hist_y, dev(x, yo, z, c))
 
     for k, src in exchange:
-        wait(R.at[src], k)
+        wait(functools.partial(R.at.__getitem__, src), k)
     rows = lax.broadcasted_iota(jnp.int32, (16, 64), 0)
     cols = lax.broadcasted_iota(jnp.int32, (16, 64), 1)
     pick = (cols == (rows - (rows & 3)) * 4 + (rows & 3)).astype(F32).astype(BF16)
     received = R[...].reshape(64, 1024)
     slab = lax.dot_general(pick, received, (((1,), (0,)), ((), ())), preferred_element_type=F32)
-    G[c, x, y, z] = slab.astype(BF16)
-
-    pos = {"x": x, "y": y, "z": z}
-    size = {"x": NX, "y": NY, "z": NZ}
+    G[c, x, y, 0] = slab.astype(BF16)
+
     whole = slice(None)
 
-    def ring(stages, pending):
-        for number, (axis, block) in enumerate(stages):
-            last = number == len(stages) - 1
-            r, n = pos[axis], size[axis]
-
-            def share(at, half):
-                if last:
-                    k = new_sem()
-                    send(block(c, at, half), block(c, at, half), k, sib)
-                    pending.append((block(oc, at, half), k))
-
-            got = []
-            for j in range(n // 2):
-                for at, half, k in got:
-                    wait(block(c, at, half), k)
-                ends = j == n // 2 - 1
-                ahead = []
-                for sign, target, half in ((1, right[axis], 0), (-1, left[axis], 1)):
-                    half = half if ends else None
-                    if ends and half == 1 and block(c, r, 1) is None:
-                        continue
-                    k = new_sem()
-                    mine = up(r, n, -sign * j)
-                    send(block(c, mine, half), block(c, mine, half), k, target)
-                    ahead.append((up(r, n, -sign * (j + 1)), half, k))
-                if j == 0:
-                    share(r, None)
-                for at, half, k in got:
-                    share(at, half)
-                got = ahead
-                yield
-            for at, half, k in got:
-                wait(block(c, at, half), k)
-                share(at, half)
-
-    def halves(half, n):
-        return whole if half is None else pl.ds(half * (n // 2), n // 2)
-
-    def z_first(columns):
-        def block(plane, at, half):
-            return None if half == 1 else G.at[plane, x, y, at, :, columns]
-        return ("z", block)
-
-    color_x = [
-        z_first(COLS_X),
-        ("y", lambda p, at, h: G.at[p, x, at, halves(h, NZ), :, COLS_X]),
-        ("x", lambda p, at, h: G.at[p, at, halves(h, NY), :, :, COLS_X]),
-    ]
-    color_y = [
-        z_first(COLS_Y),
-        ("x", lambda p, at, h: G.at[p, at, y, halves(h, NZ), :, COLS_Y]),
-        ("y", lambda p, at, h: G.at[p, halves(h, NX), at, :, :, COLS_Y]),
-    ]
-    color_z = [
-        ("x", lambda p, at, h: None if h == 1 else G.at[p, at, y, z, :, COLS_Z]),
-        ("y", lambda p, at, h: G.at[p, halves(h, NX), at, z, :, COLS_Z]),
-        ("z", lambda p, at, h: G.at[p, halves(h, NX), :, at, :, COLS_Z]),
-    ]
-    pending = []
+    def view(plane, xs, ys, slots, columns):
+        return lambda: G.at[plane, xs, ys, slots, :, columns]
+
+    def direct(axis, block):
+        n, at = (NX, x) if axis == "x" else (NY, y)
+        arrivals = []
+        for step in (1, 3, 2):
+            k = new_sem()
+            to = up(at, n, step)
+            send(block(at), block(at), k, dev(to, y, z, c) if axis == "x" else dev(x, to, z, c))
+            arrivals.append((block(up(at, n, -step)), k))
+        return arrivals
+
+    def settle(arrivals):
+        for where, k in arrivals:
+            wait(where, k)
+
+    waves = [pl.ds(0, 1), pl.ds(1, 2), pl.ds(3, 2), pl.ds(5, 2), pl.ds(7, 1)]
+
+    def second(w):
+        group_x = direct("y", lambda at: view(c, x, at, waves[w], COLS_X))
+        group_y = direct("x", lambda at: view(c, at, y, waves[w], COLS_Y))
+        return group_x, group_y
+
+    def third(w, arrivals):
+        settle(arrivals[0])
+        group_x = direct("x", lambda at: view(c, at, whole, waves[w], COLS_X))
+        settle(arrivals[1])
+        group_y = direct("y", lambda at: view(c, whole, at, waves[w], COLS_Y))
+        return group_x + group_y
+
+    zx = direct("x", lambda at: view(c, at, y, 0, COLS_Z))
+    along_z = {}
+    for off in (1, -1, 2, -2, 3, -3, 4):
+        k = new_sem()
+        send(view(c, x, y, 0, COLS_XY), view(c, x, y, SLOT[-off], COLS_XY), k, dev(x, y, up(z, NZ, off), c))
+        along_z[SLOT[-off]] = (view(c, x, y, SLOT[-off], COLS_XY), k)
+    stage2 = {0: second(0)}
+    settle(zx)
+    zy = direct("y", lambda at: view(c, whole, at, 0, COLS_Z))
+    stage3 = {0: third(0, stage2[0])}
     local[0].wait()
-    rings = [ring(color_z, pending), ring(color_x, pending), ring(color_y, pending)]
-    for run in rings:
-        next(run)
-    wait(H.at[c, x, 1 - ylo], k_hist_y)
-    hist_ring = ring([("x", lambda p, at, h: H.at[p, at] if h is None else H.at[p, at, h])], pending)
-    rings.append(hist_ring)
-    next(hist_ring)
-    for _ in range(12):
-        for run in list(rings):
-            try:
-                next(run)
-            except StopIteration:
-                rings.remove(run)
-    assert not rings
+    wait(lambda: H.at[c, x, 1 - ylo], k_hist_y)
+    settle([along_z[1], along_z[2]])
+    stage2[1] = second(1)
+    hist_x = direct("x", lambda at: lambda: H.at[c, at])
+    settle(zy)
+
+    z_right, z_left = dev(x, y, up(z, NZ, 1), c), dev(x, y, up(z, NZ, -1), c)
+    ring_sems = [(new_sem(), new_sem()) for _ in range(4)]
+    twin_sems = [new_sem() for _ in range(6)]
+
+    def ring_blocks(w):
+        xs = (whole, whole) if w < 4 else (pl.ds(0, 2), pl.ds(2, 2))
+        down, high = (2 * w - 3, 2 * w - 2) if w > 1 else (0, 0)
+        into = (2 * w - 1, 2 * w) if w < 4 else (7, 7)
+        return [
+            (view(c, xs[0], whole, down, COLS_Z), view(c, xs[0], whole, into[0], COLS_Z)),
+            (view(c, xs[1], whole, high, COLS_Z), view(c, xs[1], whole, into[1], COLS_Z)),
+        ]
+
+    def ring_send(w):
+        for (src, dst), k, target in zip(ring_blocks(w), ring_sems[w - 1], (z_right, z_left)):
+            send(src, dst, k, target)
+
+    def ring_wait(w):
+        for (_, dst), k in zip(ring_blocks(w), ring_sems[w - 1]):
+            wait(dst, k)
+
+    def twin_send(w):
+        block = view(c, whole, whole, waves[w], whole)
+        send(block, block, twin_sems[w], sib)
+
+    def twin_wait(w):
+        wait(view(oc, whole, whole, waves[w], whole), twin_sems[w])
+
+    ring_send(1)
+    stage3[1] = third(1, stage2[1])
+    settle([along_z[3], along_z[4]])
+    stage2[2] = second(2)
+    settle([along_z[5], along_z[6], along_z[7]])
+    stage2[3] = second(3)
+    stage2[4] = second(4)
+    settle(stage3[0])
+    twin_send(0)
+    stage3[2] = third(2, stage2[2])
+    settle(hist_x)
+    send(lambda: H.at[c], lambda: H.at[c], twin_sems[5], sib)
+    stage3[3] = third(3, stage2[3])
+    stage3[4] = third(4, stage2[4])
     local[1].wait()
     local[2].wait()
-    for view, k in pending:
-        wait(view, k)
+    ring_wait(1)
+    ring_send(2)
+    settle(stage3[1])
+    twin_send(1)
+    wait(lambda: H.at[oc], twin_sems[5])
+    twin_wait(0)
+    twin_wait(1)
 
     head_size = 128
     score_half = 0.5 / math.sqrt(head_size)
@@ -209,20 +229,40 @@
     for user in range(users_here):
         mask_v[user] = (event < hlen_ref[user]).astype(F32)
 
-    def head_weight(hi, zp, a, plane):
+    odd = lax.rem(z, 2)
+
+    def head_weight(hi, slots, a, plane):
         return jnp.concatenate(
-            [
-                G[plane, a + 2 * xp, hi * 2 + yl, pl.ds(2 * zp, 2)].reshape(32, 1024)
-                for xp in range(2)
-                for yl in range(2)
-            ],
+            [G[plane, a + 2 * xp, hi * 2 + yl, slot] for xp in range(2) for yl in range(2) for slot in slots],
             axis=0,
         )
 
-    def one_head(h, carry):
-        hi, zp = lax.div(h, 4), lax.rem(h, 4)
-        w_kv = jnp.concatenate([head_weight(hi, zp, 0, 0), head_weight(hi, zp, 0, 1)], axis=0)
-        w_qg = jnp.concatenate([head_weight(hi, zp, 1, 0), head_weight(hi, zp, 1, 1)], axis=0)
+    def choose(t, even_slots, odd_slots):
+        slot = jnp.int32(0)
+        for number in range(4):
+            slot = jnp.where(t == number, jnp.where(odd == 1, odd_slots[number], even_slots[number]), slot)
+        return slot
+
+    def one_head(i, carry):
+        for w in (2, 3, 4):
+            @pl.when(i == 2 * w - 3)
+            def _():
+                ring_wait(w)
+                if w < 4:
+                    ring_send(w + 1)
+                settle(stage3[w])
+                twin_send(w)
+
+            @pl.when(i == 2 * w - 2)
+            def _():
+                twin_wait(w)
+
+        t, hi = lax.div(i, 2), lax.rem(i, 2)
+        turn = t + lax.div(t, 2) - 2 * lax.div(t, 3)
+        h = hi * 4 + lax.rem(lax.div(z, 2) + (2 * odd - 1) * turn + 8, 4)
+        slots = (choose(t, (0, 3, 4, 7), (1, 2, 5, 6)), choose(t, (2, 1, 6, 5), (0, 4, 3, 7)))
+        w_kv = jnp.concatenate([head_weight(hi, slots, 0, 0), head_weight(hi, slots, 0, 1)], axis=0)
+        w_qg = jnp.concatenate([head_weight(hi, slots, 1, 0), head_weight(hi, slots, 1, 1)], axis=0)
         at = pl.ds(pl.multiple_of(h * 128, 128), 128)
         for user in range(users_here):
             rows_c = cand_v[user]
@@ -277,8 +317,8 @@
         pltpu.make_async_copy(out_v.at[user], out_ref.at[user], local_sem.at[3 + user]).start()
     for user in range(users_here):
         pltpu.make_async_copy(out_v.at[user], out_ref.at[user], local_sem.at[3 + user]).wait()
-    for copy in sent:
-        copy.wait_send()
+    for src, k in sent:
+        rcopy(src, src, k, sib).wait_send()
     assert state["k"] <= NSEM
 
 

time: 88.7 us -> 74.8 us (0.84)
  Pallas kernels: 85.9 us -> 71.9 us
    pallas_call x1, Pallas kernels: 85.9 us -> 71.9 us  [body(): pl.pallas_call(kernel, out_shape=jax.ShapeDtypeStruct(candidates.shape, B...]
where the time goes in v2:
time: 74.8 us; the launch traced here: 74.6 us
  Pallas kernels  71.9 us (96%)
  local copies, waits for them, and re-layouts  2.67 us (4%)
    pallas_call x1, Pallas kernels, body(): pl.pallas_call(kernel, out_shape=jax.ShapeDtypeStruct(candidates.shape, B...  71.9 us
    unnamed x1, local copies, waits for them, and re-layouts  2.67 us

profile of v2, /device:TPU:1, one launch (start us, length us, event | category | flops | bytes accessed | tf_op | source)
XLA Modules:
  0.0 74.6 jit_solution(5233813147284383604)
XLA Ops:
  0.0 71.9 %shard_map.64 = bf16[2,384,1024]{2,1,0:T(8,128)(2,1)} custom-call(bf16[2,384,1024]{2,1,0:T(8,128)(2,1)} %cand_ref.1, bf16[2,32,1024]{2,1,0:T(8,128)(2,1)} %hist_ref.1, bf16[4,4,1024]{2,1,0:T(4,128)(2,1)} %proj_ref.1, bf16[1024,1024]{1,0:T(8,128)(2,1)} %ow_ref.1, s32[2]{0:T(128)} %hlen_ref.1, s32[2]{0:T(128)} %ccount_ref.1), custom_call_target="tpu_custom_call" | custom-call | tf_op jit(solution)/shard_map/pallas_call | solution.py:329
  71.9 2.7 %copy.8 = bf16[2,384,1024]{2,1,0:T(8,128)(2,1)} copy(bf16[2,384,1024]{2,1,0:T(8,128)(2,1)} %shard_map.64) | data formatting | bytes 3145728

commit v3 on v2

v3 whole, which is shorter than its diff:
```python
import math

import jax
import jax.numpy as jnp
from jax import lax
from jax.experimental import pallas as pl
from jax.experimental.pallas import tpu as pltpu
from jax.sharding import PartitionSpec as P

MESH = pl.DeviceIdType.MESH
HEADS = 8
NX, NY, NZ = 4, 4, 8
BF16, F32 = jnp.bfloat16, jnp.float32
COLS_X, COLS_Y, COLS_Z = pl.ds(0, 256), pl.ds(256, 384), pl.ds(640, 384)
COLS_XY = pl.ds(0, 640)
SLOT = {0: 0, -1: 1, 1: 2, -2: 3, 2: 4, -3: 5, 3: 6, 4: 7, -4: 7}
NSEM = 128


def nt_dot(a, b):
    return lax.dot_general(a, b, (((1,), (1,)), ((), ())), preferred_element_type=F32)


def half_silu(t):
    return t + t * jnp.tanh(t)


def kernel(
    cand_ref, hist_ref, proj_ref, ow_ref, hlen_ref, ccount_ref, out_ref,
    G, H, KV, W, pick_v, cand_v, ow_v, mask_v, attn, gate, gated, out_v, send_sem, recv_sem, local_sem,
):
    u = lax.axis_index("users")
    s = lax.axis_index("score")
    z = lax.rem(u, NZ)
    yhi = lax.div(u, NZ)
    c = lax.rem(s, 2)
    x = lax.rem(lax.div(s, 2), NX)
    ylo = lax.div(s, 8)
    y = yhi * 2 + ylo
    oc = 1 - c

    def dev(px, py, pz, pc):
        return (lax.div(py, 2) * NZ + pz, lax.rem(py, 2) * 8 + px * 2 + pc)

    def up(pos, n, k):
        return lax.rem(pos + k + n, n)

    yo = y + 1 - 2 * ylo
    sib = dev(x, y, z, oc)
    local = [
        pltpu.make_async_copy(hist_ref.at[c], H.at[x, ylo, c], local_sem.at[0]),
        pltpu.make_async_copy(cand_ref, cand_v, local_sem.at[1]),
        pltpu.make_async_copy(ow_ref, ow_v, local_sem.at[2]),
    ]
    for copy in local:
        copy.start()

    barrier = pltpu.get_barrier_semaphore()
    partners = [dev(up(x, NX, k), y, z, c) for k in (1, 3, 2)] + [dev(x, up(y, NY, k), z, c) for k in (1, 3, 2)]
    partners += [dev(x, y, up(z, NZ, k), c) for k in (1, 7, 2, 6, 3, 5, 4)] + [sib]
    for partner in partners:
        pl.semaphore_signal(barrier, inc=1, device_id=partner, device_id_type=MESH)

    row16 = lax.broadcasted_iota(jnp.int32, (16, 1024), 0)
    tile = jnp.zeros((16, 1024), F32)
    for f in range(4):
        rows_f = proj_ref[f].astype(F32)
        for p in range(4):
            tile = jnp.where(row16 == f * 4 + p, jnp.broadcast_to(rows_f[p : p + 1], (16, 1024)), tile)
    G[c, x, y, 0] = tile.astype(BF16)

    pl.semaphore_wait(barrier, len(partners))

    state = {"k": 0}
    sent = []

    def new_sem():
        k = state["k"]
        state["k"] = k + 1
        return k

    def rcopy(src, dst, k, target):
        return pltpu.make_async_remote_copy(
            src_ref=src(), dst_ref=dst(), send_sem=send_sem.at[k], recv_sem=recv_sem.at[k],
            device_id=target, device_id_type=MESH,
        )

    def send(src, dst, k, target):
        rcopy(src, dst, k, target).start()
        sent.append((src, k))

    def wait(dst, k):
        rcopy(dst, dst, k, sib).wait_recv()

    k_hist_c = new_sem()
    send(lambda: hist_ref.at[oc], lambda: H.at[x, ylo, c], k_hist_c, sib)

    whole = slice(None)

    def view(plane, xs, ys, slots, columns):
        return lambda: G.at[plane, xs, ys, slots, :, columns]

    def direct(axis, block):
        n, at = (NX, x) if axis == "x" else (NY, y)
        arrivals = []
        for step in (1, 3, 2):
            k = new_sem()
            to = up(at, n, step)
            send(block(at), block(at), k, dev(to, y, z, c) if axis == "x" else dev(x, to, z, c))
            arrivals.append((block(up(at, n, -step)), k))
        return arrivals

    def settle(arrivals):
        for where, k in arrivals:
            wait(where, k)

    waves = [pl.ds(0, 1), pl.ds(1, 2), pl.ds(3, 2), pl.ds(5, 2), pl.ds(7, 1)]

    def second(w):
        group_x = direct("y", lambda at: view(c, x, at, waves[w], COLS_X))
        group_y = direct("x", lambda at: view(c, at, y, waves[w], COLS_Y))
        return group_x, group_y

    def third(w, arrivals):
        settle(arrivals[0])
        group_x = direct("x", lambda at: view(c, at, whole, waves[w], COLS_X))
        settle(arrivals[1])
        group_y = direct("y", lambda at: view(c, whole, at, waves[w], COLS_Y))
        return group_x + group_y

    spot = {"x": [up(x, NX, k) for k in range(NX)], "y": [up(y, NY, k) for k in range(NY)]}
    neighbour = {
        "x": [dev(spot["x"][k], y, z, c) for k in range(NX)],
        "y": [dev(x, spot["y"][k], z, c) for k in range(NY)],
    }

    def ring_first(axis, block):
        arrivals = []
        for step in (1, 3):
            k = new_sem()
            send(block(spot[axis][0], None), block(spot[axis][0], None), k, neighbour[axis][step])
            arrivals.append((block(spot[axis][4 - step], None), k))
        sems = [new_sem(), new_sem()]
        return arrivals, sems, [(block(spot[axis][2], half), sems[half]) for half in range(2)]

    def ring_second(axis, block, started):
        settle(started[0])
        for half, step in ((0, 1), (1, 3)):
            mine = block(spot[axis][4 - step], half)
            send(mine, mine, started[1][half], neighbour[axis][step])
        return started[2]

    def part(half):
        return whole if half is None else pl.ds(2 * half, 2)

    def wave_x(w):
        return "x", lambda at, half: view(c, at, part(half), waves[w], COLS_X)

    def wave_y(w):
        return "y", lambda at, half: view(c, part(half), at, waves[w], COLS_Y)

    def third_first(w, arrivals):
        settle(arrivals[0])
        group_x = ring_first(*wave_x(w))
        settle(arrivals[1])
        group_y = ring_first(*wave_y(w))
        return group_x, group_y

    def third_second(w):
        ring_second(*wave_x(w), stage3[w][0])
        ring_second(*wave_y(w), stage3[w][1])

    def hist_block(at, half):
        return (lambda: H.at[at]) if half is None else (lambda: H.at[at, half])

    zx = direct("x", lambda at: view(c, at, y, 0, COLS_Z))
    along_z = {}
    for off in (1, -1, 2, -2, 3, -3, 4):
        k = new_sem()
        send(view(c, x, y, 0, COLS_XY), view(c, x, y, SLOT[-off], COLS_XY), k, dev(x, y, up(z, NZ, off), c))
        along_z[SLOT[-off]] = (view(c, x, y, SLOT[-off], COLS_XY), k)
    stage2 = {0: second(0)}
    local[0].wait()
    wait(lambda: H.at[x, ylo, oc], k_hist_c)
    k_hist_y = new_sem()
    send(lambda: H.at[x, ylo], lambda: H.at[x, ylo], k_hist_y, dev(x, yo, z, c))
    settle(zx)
    zy = direct("y", lambda at: view(c, whole, at, 0, COLS_Z))
    stage3 = {0: third(0, stage2[0])}
    wait(lambda: H.at[x, 1 - ylo], k_hist_y)
    hist_x = ring_first("x", hist_block)
    settle([along_z[1], along_z[2]])
    stage2[1] = second(1)
    settle(zy)

    z_right, z_left = dev(x, y, up(z, NZ, 1), c), dev(x, y, up(z, NZ, -1), c)
    ring_sems = [(new_sem(), new_sem()) for _ in range(4)]
    twin_sems = [new_sem() for _ in range(5)]
    kv_sems = [new_sem() for _ in range(HEADS)]

    def ring_blocks(w):
        xs = (whole, whole) if w < 4 else (pl.ds(0, 2), pl.ds(2, 2))
        down, high = (2 * w - 3, 2 * w - 2) if w > 1 else (0, 0)
        into = (2 * w - 1, 2 * w) if w < 4 else (7, 7)
        return [
            (view(c, xs[0], whole, down, COLS_Z), view(c, xs[0], whole, into[0], COLS_Z)),
            (view(c, xs[1], whole, high, COLS_Z), view(c, xs[1], whole, into[1], COLS_Z)),
        ]

    def ring_send(w):
        for (src, dst), k, target in zip(ring_blocks(w), ring_sems[w - 1], (z_right, z_left)):
            send(src, dst, k, target)

    def ring_wait(w):
        for (_, dst), k in zip(ring_blocks(w), ring_sems[w - 1]):
            wait(dst, k)

    def twin_send(w):
        block = view(c, whole, whole, waves[w], whole)
        send(block, block, twin_sems[w], sib)

    def twin_wait(w):
        wait(view(oc, whole, whole, waves[w], whole), twin_sems[w])

    ring_send(1)
    stage3[1] = third(1, stage2[1])
    settle([along_z[3], along_z[4]])
    stage2[2] = second(2)
    hist_x = ring_second("x", hist_block, hist_x)
    settle([along_z[5], along_z[6], along_z[7]])
    stage2[3] = second(3)
    stage2[4] = second(4)
    settle(stage3[0])
    twin_send(0)
    stage3[2] = third_first(2, stage2[2])
    stage3[3] = third_first(3, stage2[3])
    stage3[4] = third_first(4, stage2[4])
    local[1].wait()
    local[2].wait()
    ring_wait(1)
    ring_send(2)
    settle(stage3[1])
    twin_send(1)
    third_second(2)
    settle(hist_x)
    twin_wait(0)
    twin_wait(1)

    head_size = 128
    score_half = 0.5 / math.sqrt(head_size)
    users_here = cand_v.shape[0]

    q = lax.broadcasted_iota(jnp.int32, (512, 128), 0)
    event = (((q >> 6) & 1) * 8 + (q >> 7) * 2 + ((q >> 5) & 1)) * 32 + (q & 31)
    mask_v[...] = (event < hlen_ref[c]).astype(F32)
    out_row = lax.broadcasted_iota(jnp.int32, (256, 256), 0)
    in_row = lax.broadcasted_iota(jnp.int32, (256, 256), 1)
    source = ((out_row & 63) >> 2) * 16 + (out_row & 3) * 4 + (out_row >> 6)
    pick_v[...] = (in_row == source).astype(F32).astype(BF16)

    odd = lax.rem(z, 2)

    def slabs(hi, slot):
        return jnp.concatenate(
            [G[plane, px, hi * 2 + yl, slot] for yl in range(2) for px in range(NX) for plane in range(2)],
            axis=0,
        )

    def choose(t, even_slots, odd_slots):
        slot = jnp.int32(0)
        for number in range(4):
            slot = jnp.where(t == number, jnp.where(odd == 1, odd_slots[number], even_slots[number]), slot)
        return slot

    def chunk(t, carry):
        for w in (2, 3, 4):
            @pl.when(t == w - 1)
            def _():
                twin_wait(w)

        turn = t + lax.div(t, 2) - 2 * lax.div(t, 3)
        pair = lax.rem(lax.div(z, 2) + (2 * odd - 1) * turn + 8, 4)
        slots = (choose(t, (0, 3, 4, 7), (1, 2, 5, 6)), choose(t, (2, 1, 6, 5), (0, 4, 3, 7)))

        def keys_values(hi, carry):
            for zl in range(2):
                sorted_rows = jnp.dot(pick_v[...], slabs(hi, slots[zl]), preferred_element_type=F32).astype(BF16)
                for p in range(4):
                    W[hi, p, zl * 64 : zl * 64 + 64] = sorted_rows[p * 64 : p * 64 + 64]
            kv = half_silu(0.5 * nt_dot(H[...].reshape(512, 1024), W[hi, 0:2].reshape(256, 1024)))
            KV[t, hi, c, :, :128] = kv[:, :128].astype(BF16)
            KV[t, hi, c, :, 128:] = (kv[:, 128:] * mask_v[...]).astype(BF16)
            kv_copy(t, hi, c).start()
            return carry

        lax.fori_loop(0, 2, keys_values, 0)

        def attend(hi, carry):
            for w in (3, 4):
                @pl.when((t == w - 3) & (hi == 0))
                def _():
                    third_second(w)

            for w in (2, 3, 4):
                @pl.when((t == w - 2) & (hi == 1))
                def _():
                    ring_wait(w)
                    if w < 4:
                        ring_send(w + 1)
                    settle(stage3[w][0][2] + stage3[w][1][2])
                    twin_send(w)

            kv_copy(t, hi, oc).wait_recv()
            h = hi * 4 + pair
            at = pl.ds(pl.multiple_of(h * 128, 128), 128)
            for user in range(users_here):
                rows_c = cand_v[user]
                qg = half_silu(0.5 * nt_dot(rows_c, W[hi, 2:4].reshape(256, 1024))).astype(BF16)
                kv_c = half_silu(0.5 * nt_dot(rows_c, W[hi, 0:2].reshape(256, 1024))).astype(BF16)
                queries = qg[:, :128]
                gate[user, :, at] = qg[:, 128:]
                keys, values = KV[t, hi, user, :, :128], KV[t, hi, user, :, 128:]
                weights = half_silu(nt_dot(queries, keys) * score_half).astype(BF16)
                att = jnp.dot(weights, values, preferred_element_type=F32)
                own = jnp.sum(queries.astype(F32) * kv_c[:, :128].astype(F32), axis=1, keepdims=True)
                own = half_silu(own * score_half)
                attn[user, :, at] = att + own * kv_c[:, 128:].astype(F32)
            return carry

        lax.fori_loop(0, 2, attend, 0)
        return carry

    def kv_copy(t, hi, whose):
        k = kv_sems[0] + t * 2 + hi
        return pltpu.make_async_remote_copy(
            src_ref=KV.at[t, hi, whose], dst_ref=KV.at[t, hi, whose],
            send_sem=send_sem.at[k], recv_sem=recv_sem.at[k], device_id=sib, device_id_type=MESH,
        )

    lax.fori_loop(0, HEADS // 2, chunk, 0)

    slot0 = s * 384

    def norm(user, block):
        rows_a = attn[user, block]
        mean = jnp.sum(rows_a, axis=1, keepdims=True) * (1.0 / 1024)
        centered = rows_a - mean
        var = jnp.sum(centered * centered, axis=1, keepdims=True) * (1.0 / 1024)
        normed = centered * lax.rsqrt(var + 1e-06)
        gated[user, block] = (normed * gate[user, block].astype(F32)).astype(BF16)

    def norm_step(i, carry):
        norm(0, pl.ds(pl.multiple_of(i * 64, 64), 64))
        return carry

    lax.fori_loop(0, 6, norm_step, 0)
    for user in range(users_here):
        for n in range(4):
            ncols = pl.ds(n * 256, 256)
            mixed = jnp.dot(gated[user], ow_v[:, ncols], preferred_element_type=F32)
            mixed = mixed + cand_v[user, :, ncols].astype(F32)
            slot = slot0 + lax.broadcasted_iota(jnp.int32, (384, 256), 0)
            out_v[user, :, ncols] = jnp.where(slot < ccount_ref[user], mixed, 0.0).astype(BF16)
            if user == 0:
                for piece in range(3):
                    norm(1, pl.ds(n * 96 + piece * 32, 32))
        pltpu.make_async_copy(out_v.at[user], out_ref.at[user], local_sem.at[3 + user]).start()
    for user in range(users_here):
        pltpu.make_async_copy(out_v.at[user], out_ref.at[user], local_sem.at[3 + user]).wait()
    for number in range(HEADS):
        kv_copy(number // 2, number % 2, c).wait_send()
    for src, k in sent:
        rcopy(src, src, k, sib).wait_send()
    assert state["k"] <= NSEM


def body(candidates, history, proj_weight, out_weight, hist_len, cand_count):
    anyspace = pl.BlockSpec(memory_space=pl.ANY)
    smem = pl.BlockSpec(memory_space=pltpu.SMEM)
    vmem = pl.BlockSpec(memory_space=pltpu.VMEM)
    return pl.pallas_call(
        kernel,
        out_shape=jax.ShapeDtypeStruct(candidates.shape, BF16),
        in_specs=[anyspace, anyspace, vmem, anyspace, smem, smem],
        out_specs=anyspace,
        scratch_shapes=[
            pltpu.VMEM((2, NX, NY, NZ, 16, 1024), BF16),
            pltpu.VMEM((NX, 2, 2, 32, 1024), BF16),
            pltpu.VMEM((4, 2, 2, 512, 256), BF16),
            pltpu.VMEM((2, 4, 128, 1024), BF16),
            pltpu.VMEM((256, 256), BF16),
            pltpu.VMEM((2, 384, 1024), BF16),
            pltpu.VMEM((1024, 1024), BF16),
            pltpu.VMEM((512, 128), F32),
            pltpu.VMEM((2, 384, 1024), F32),
            pltpu.VMEM((2, 384, 1024), BF16),
            pltpu.VMEM((2, 384, 1024), BF16),
            pltpu.VMEM((2, 384, 1024), BF16),
            pltpu.SemaphoreType.DMA((NSEM,)),
            pltpu.SemaphoreType.DMA((NSEM,)),
            pltpu.SemaphoreType.DMA((5,)),
        ],
        compiler_params=pltpu.CompilerParams(
            collective_id=0, has_side_effects=True, vmem_limit_bytes=56 * 1024 * 1024
        ),
    )(candidates, history, proj_weight, out_weight, hist_len, cand_count)


def solution(mesh):
    in_specs = (
        P("users", "score", None),
        P("users", "score", None),
        P(("users", "score"), None, None),
        P(),
        P("users"),
        P("users"),
    )
    out_specs = P("users", "score", None)
    return jax.shard_map(body, mesh=mesh, in_specs=in_specs, out_specs=out_specs, check_vma=False)
```

time: 74.8 us -> 74.5 us (level)
  no operation moved by 1% of the time
where the time goes in v3:
time: 74.5 us; the launch traced here: 74.3 us
  Pallas kernels  71.6 us (96%)
  local copies, waits for them, and re-layouts  2.67 us (4%)
    pallas_call x1, Pallas kernels, body(): pl.pallas_call(kernel, out_shape=jax.ShapeDtypeStruct(candidates.shape, B...  71.6 us
    unnamed x1, local copies, waits for them, and re-layouts  2.67 us

profile of v3, /device:TPU:1, one launch (start us, length us, event | category | flops | bytes accessed | tf_op | source)
XLA Modules:
  0.0 74.3 jit_solution(13424764427443012057)
XLA Ops:
  0.0 71.6 %shard_map.64 = bf16[2,384,1024]{2,1,0:T(8,128)(2,1)} custom-call(bf16[2,384,1024]{2,1,0:T(8,128)(2,1)} %cand_ref.1, bf16[2,32,1024]{2,1,0:T(8,128)(2,1)} %hist_ref.1, bf16[4,4,1024]{2,1,0:T(4,128)(2,1)} %proj_ref.1, bf16[1024,1024]{1,0:T(8,128)(2,1)} %ow_ref.1, s32[2]{0:T(128)} %hlen_ref.1, s32[2]{0:T(128)} %ccount_ref.1), custom_call_target="tpu_custom_call" | custom-call | tf_op jit(solution)/shard_map/pallas_call | solution.py:381
  71.6 2.7 %copy.8 = bf16[2,384,1024]{2,1,0:T(8,128)(2,1)} copy(bf16[2,384,1024]{2,1,0:T(8,128)(2,1)} %shard_map.64) | data formatting | bytes 3145728

commit v4 on v3

--- a/solution.py
+++ b/solution.py
@@ -1,3 +1,4 @@
+import functools
 import math
 
 import jax
@@ -57,7 +58,7 @@
 
     barrier = pltpu.get_barrier_semaphore()
     partners = [dev(up(x, NX, k), y, z, c) for k in (1, 3, 2)] + [dev(x, up(y, NY, k), z, c) for k in (1, 3, 2)]
-    partners += [dev(x, y, up(z, NZ, k), c) for k in (1, 7, 2, 6, 3, 5, 4)] + [sib]
+    partners += [dev(x, y, up(z, NZ, k), c) for k in (1, 7, 2, 6, 3, 5, 4)] + [sib, dev(x, yo, z, oc)]
     for partner in partners:
         pl.semaphore_signal(barrier, inc=1, device_id=partner, device_id_type=MESH)
 
@@ -92,8 +93,13 @@
     def wait(dst, k):
         rcopy(dst, dst, k, sib).wait_recv()
 
-    k_hist_c = new_sem()
-    send(lambda: hist_ref.at[oc], lambda: H.at[x, ylo, c], k_hist_c, sib)
+    hist_arrivals = []
+    for who, target, py, pc in (
+        (oc, sib, ylo, oc), (c, dev(x, yo, z, c), 1 - ylo, c), (oc, dev(x, yo, z, oc), 1 - ylo, oc),
+    ):
+        k = new_sem()
+        send(functools.partial(hist_ref.at.__getitem__, who), lambda: H.at[x, ylo, c], k, target)
+        hist_arrivals.append((functools.partial(H.at.__getitem__, (x, py, pc)), k))
 
     whole = slice(None)
 
@@ -134,21 +140,19 @@
         "y": [dev(x, spot["y"][k], z, c) for k in range(NY)],
     }
 
-    def ring_first(axis, block):
-        arrivals = []
-        for step in (1, 3):
-            k = new_sem()
+    def ring_plan(axis, block):
+        first = [(block(spot[axis][3], None), new_sem()), (block(spot[axis][1], None), new_sem())]
+        return first, [(block(spot[axis][2], half), new_sem()) for half in range(2)]
+
+    def ring_first(axis, block, plan):
+        for (_, k), step in zip(plan[0], (1, 3)):
             send(block(spot[axis][0], None), block(spot[axis][0], None), k, neighbour[axis][step])
-            arrivals.append((block(spot[axis][4 - step], None), k))
-        sems = [new_sem(), new_sem()]
-        return arrivals, sems, [(block(spot[axis][2], half), sems[half]) for half in range(2)]
-
-    def ring_second(axis, block, started):
-        settle(started[0])
+
+    def ring_second(axis, block, plan):
+        settle(plan[0])
         for half, step in ((0, 1), (1, 3)):
             mine = block(spot[axis][4 - step], half)
-            send(mine, mine, started[1][half], neighbour[axis][step])
-        return started[2]
+            send(mine, mine, plan[1][half][1], neighbour[axis][step])
 
     def part(half):
         return whole if half is None else pl.ds(2 * half, 2)
@@ -159,36 +163,41 @@
     def wave_y(w):
         return "y", lambda at, half: view(c, part(half), at, waves[w], COLS_Y)
 
-    def third_first(w, arrivals):
-        settle(arrivals[0])
-        group_x = ring_first(*wave_x(w))
-        settle(arrivals[1])
-        group_y = ring_first(*wave_y(w))
-        return group_x, group_y
+    plans = {w: (ring_plan(*wave_x(w)), ring_plan(*wave_y(w))) for w in (2, 3, 4)}
+
+    def third_first(w):
+        settle(stage2[w][0])
+        ring_first(*wave_x(w), plans[w][0])
+        settle(stage2[w][1])
+        ring_first(*wave_y(w), plans[w][1])
 
     def third_second(w):
-        ring_second(*wave_x(w), stage3[w][0])
-        ring_second(*wave_y(w), stage3[w][1])
+        ring_second(*wave_x(w), plans[w][0])
+        ring_second(*wave_y(w), plans[w][1])
 
     def hist_block(at, half):
         return (lambda: H.at[at]) if half is None else (lambda: H.at[at, half])
 
-    zx = direct("x", lambda at: view(c, at, y, 0, COLS_Z))
+    hist_plan = ring_plan("x", hist_block)
     along_z = {}
-    for off in (1, -1, 2, -2, 3, -3, 4):
+
+    def z_send(off):
         k = new_sem()
         send(view(c, x, y, 0, COLS_XY), view(c, x, y, SLOT[-off], COLS_XY), k, dev(x, y, up(z, NZ, off), c))
         along_z[SLOT[-off]] = (view(c, x, y, SLOT[-off], COLS_XY), k)
+
+    zx = direct("x", lambda at: view(c, at, y, 0, COLS_Z))
+    z_send(1)
+    z_send(-1)
     stage2 = {0: second(0)}
+    for off in (2, -2, 3, -3, 4):
+        z_send(off)
     local[0].wait()
-    wait(lambda: H.at[x, ylo, oc], k_hist_c)
-    k_hist_y = new_sem()
-    send(lambda: H.at[x, ylo], lambda: H.at[x, ylo], k_hist_y, dev(x, yo, z, c))
+    settle(hist_arrivals)
+    ring_first("x", hist_block, hist_plan)
     settle(zx)
     zy = direct("y", lambda at: view(c, whole, at, 0, COLS_Z))
     stage3 = {0: third(0, stage2[0])}
-    wait(lambda: H.at[x, 1 - ylo], k_hist_y)
-    hist_x = ring_first("x", hist_block)
     settle([along_z[1], along_z[2]])
     stage2[1] = second(1)
     settle(zy)
@@ -226,23 +235,21 @@
     stage3[1] = third(1, stage2[1])
     settle([along_z[3], along_z[4]])
     stage2[2] = second(2)
-    hist_x = ring_second("x", hist_block, hist_x)
-    settle([along_z[5], along_z[6], along_z[7]])
-    stage2[3] = second(3)
-    stage2[4] = second(4)
+    ring_second("x", hist_block, hist_plan)
     settle(stage3[0])
     twin_send(0)
-    stage3[2] = third_first(2, stage2[2])
-    stage3[3] = third_first(3, stage2[3])
-    stage3[4] = third_first(4, stage2[4])
-    local[1].wait()
-    local[2].wait()
+    third_first(2)
     ring_wait(1)
     ring_send(2)
     settle(stage3[1])
     twin_send(1)
+    settle([along_z[5], along_z[6], along_z[7]])
+    stage2[3] = second(3)
+    stage2[4] = second(4)
     third_second(2)
-    settle(hist_x)
+    local[1].wait()
+    local[2].wait()
+    settle(hist_plan[1])
     twin_wait(0)
     twin_wait(1)
 
@@ -296,24 +303,30 @@
         lax.fori_loop(0, 2, keys_values, 0)
 
         def attend(hi, carry):
-            for w in (3, 4):
-                @pl.when((t == w - 3) & (hi == 0))
-                def _():
-                    third_second(w)
+            @pl.when((t == 0) & (hi == 0))
+            def _():
+                third_first(3)
+                third_first(4)
+
+            @pl.when((t == 0) & (hi == 1))
+            def _():
+                third_second(3)
+                third_second(4)
 
             for w in (2, 3, 4):
-                @pl.when((t == w - 2) & (hi == 1))
+                @pl.when((t == w - 2) & (hi == 0))
                 def _():
                     ring_wait(w)
                     if w < 4:
                         ring_send(w + 1)
-                    settle(stage3[w][0][2] + stage3[w][1][2])
+                    settle(plans[w][0][1] + plans[w][1][1])
                     twin_send(w)
 
-            kv_copy(t, hi, oc).wait_recv()
             h = hi * 4 + pair
             at = pl.ds(pl.multiple_of(h * 128, 128), 128)
-            for user in range(users_here):
+            for user in (c, oc):
+                if user is oc:
+                    kv_copy(t, hi, oc).wait_recv()
                 rows_c = cand_v[user]
                 qg = half_silu(0.5 * nt_dot(rows_c, W[hi, 2:4].reshape(256, 1024))).astype(BF16)
                 kv_c = half_silu(0.5 * nt_dot(rows_c, W[hi, 0:2].reshape(256, 1024))).astype(BF16)

time: 74.5 us -> 75.7 us (1.016)
  Pallas kernels: 71.6 us -> 72.8 us
    pallas_call x1, Pallas kernels: 71.6 us -> 72.8 us  [body(): pl.pallas_call(kernel, out_shape=jax.ShapeDtypeStruct(candidates.shape, B...]
where the time goes in v4:
time: 75.7 us; the launch traced here: 75.5 us
  Pallas kernels  72.8 us (96%)
  local copies, waits for them, and re-layouts  2.67 us (4%)
    pallas_call x1, Pallas kernels, body(): pl.pallas_call(kernel, out_shape=jax.ShapeDtypeStruct(candidates.shape, B...  72.8 us
    unnamed x1, local copies, waits for them, and re-layouts  2.67 us

profile of v4, /device:TPU:1, one launch (start us, length us, event | category | flops | bytes accessed | tf_op | source)
XLA Modules:
  0.0 75.5 jit_solution(11591820835920165739)
XLA Ops:
  0.0 72.8 %shard_map.64 = bf16[2,384,1024]{2,1,0:T(8,128)(2,1)} custom-call(bf16[2,384,1024]{2,1,0:T(8,128)(2,1)} %cand_ref.1, bf16[2,32,1024]{2,1,0:T(8,128)(2,1)} %hist_ref.1, bf16[4,4,1024]{2,1,0:T(4,128)(2,1)} %proj_ref.1, bf16[1024,1024]{1,0:T(8,128)(2,1)} %ow_ref.1, s32[2]{0:T(128)} %hlen_ref.1, s32[2]{0:T(128)} %ccount_ref.1), custom_call_target="tpu_custom_call" | custom-call | tf_op jit(solution)/shard_map/pallas_call | solution.py:394
  72.8 2.7 %copy.8 = bf16[2,384,1024]{2,1,0:T(8,128)(2,1)} copy(bf16[2,384,1024]{2,1,0:T(8,128)(2,1)} %shard_map.64) | data formatting | bytes 3145728

commit v5 on v4

--- a/solution.py
+++ b/solution.py
@@ -28,7 +28,7 @@
 
 def kernel(
     cand_ref, hist_ref, proj_ref, ow_ref, hlen_ref, ccount_ref, out_ref,
-    G, H, KV, W, pick_v, cand_v, ow_v, mask_v, attn, gate, gated, out_v, send_sem, recv_sem, local_sem,
+    G, H, KV, Q, W, pick_v, cand_v, ow_v, mask_v, attn, gate, gated, out_v, send_sem, recv_sem, local_sem,
 ):
     u = lax.axis_index("users")
     s = lax.axis_index("score")
@@ -192,9 +192,6 @@
     stage2 = {0: second(0)}
     for off in (2, -2, 3, -3, 4):
         z_send(off)
-    local[0].wait()
-    settle(hist_arrivals)
-    ring_first("x", hist_block, hist_plan)
     settle(zx)
     zy = direct("y", lambda at: view(c, whole, at, 0, COLS_Z))
     stage3 = {0: third(0, stage2[0])}
@@ -233,23 +230,24 @@
 
     ring_send(1)
     stage3[1] = third(1, stage2[1])
+    local[0].wait()
+    settle(hist_arrivals)
+    ring_first("x", hist_block, hist_plan)
     settle([along_z[3], along_z[4]])
     stage2[2] = second(2)
-    ring_second("x", hist_block, hist_plan)
     settle(stage3[0])
     twin_send(0)
-    third_first(2)
+    settle([along_z[5], along_z[6], along_z[7]])
+    stage2[3] = second(3)
+    stage2[4] = second(4)
     ring_wait(1)
     ring_send(2)
     settle(stage3[1])
     twin_send(1)
-    settle([along_z[5], along_z[6], along_z[7]])
-    stage2[3] = second(3)
-    stage2[4] = second(4)
-    third_second(2)
+    third_first(2)
+    ring_second("x", hist_block, hist_plan)
     local[1].wait()
     local[2].wait()
-    settle(hist_plan[1])
     twin_wait(0)
     twin_wait(1)
 
@@ -279,68 +277,93 @@
             slot = jnp.where(t == number, jnp.where(odd == 1, odd_slots[number], even_slots[number]), slot)
         return slot
 
+    def pair_of(t):
+        turn = t + lax.div(t, 2) - 2 * lax.div(t, 3)
+        return lax.rem(lax.div(z, 2) + (2 * odd - 1) * turn + 8, 4)
+
+    def columns_of(t, hi):
+        return pl.ds(pl.multiple_of((hi * 4 + pair_of(t)) * 128, 128), 128)
+
+    def project(t, hi):
+        slots = (choose(t, (0, 3, 4, 7), (1, 2, 5, 6)), choose(t, (2, 1, 6, 5), (0, 4, 3, 7)))
+        keep, at = lax.rem(t, 2), columns_of(t, hi)
+        for zl in range(2):
+            sorted_rows = jnp.dot(pick_v[...], slabs(hi, slots[zl]), preferred_element_type=F32).astype(BF16)
+            for p in range(4):
+                W[keep, hi, p, zl * 64 : zl * 64 + 64] = sorted_rows[p * 64 : p * 64 + 64]
+        for user in range(users_here):
+            rows_c = cand_v[user]
+            qg = half_silu(0.5 * nt_dot(rows_c, W[keep, hi, 2:4].reshape(256, 1024))).astype(BF16)
+            kv_c = half_silu(0.5 * nt_dot(rows_c, W[keep, hi, 0:2].reshape(256, 1024))).astype(BF16)
+            queries = qg[:, :128]
+            Q[keep, hi, user] = queries
+            gate[user, :, at] = qg[:, 128:]
+            own = jnp.sum(queries.astype(F32) * kv_c[:, :128].astype(F32), axis=1, keepdims=True)
+            attn[user, :, at] = half_silu(own * score_half) * kv_c[:, 128:].astype(F32)
+
+    def keys_values(t, hi):
+        w_kv = W[lax.rem(t, 2), hi, 0:2].reshape(256, 1024)
+        kv = half_silu(0.5 * nt_dot(H[...].reshape(512, 1024), w_kv))
+        KV[t, hi, c, :, :128] = kv[:, :128].astype(BF16)
+        KV[t, hi, c, :, 128:] = (kv[:, 128:] * mask_v[...]).astype(BF16)
+        kv_copy(t, hi, c).start()
+
+    def attend(t, hi):
+        kv_copy(t, hi, oc).wait_recv()
+        keep, at = lax.rem(t, 2), columns_of(t, hi)
+        for user in range(users_here):
+            keys, values = KV[t, hi, user, :, :128], KV[t, hi, user, :, 128:]
+            weights = half_silu(nt_dot(Q[keep, hi, user], keys) * score_half).astype(BF16)
+            attn[user, :, at] += jnp.dot(weights, values, preferred_element_type=F32)
+
+    def both(work, t):
+        def step(hi, carry):
+            work(t, hi)
+            return carry
+
+        lax.fori_loop(0, 2, step, 0)
+
     def chunk(t, carry):
+        @pl.when(t == 1)
+        def _():
+            settle(hist_plan[1])
+
+        @pl.when(t > 0)
+        def _():
+            both(keys_values, t - 1)
+
         for w in (2, 3, 4):
             @pl.when(t == w - 1)
             def _():
                 twin_wait(w)
 
-        turn = t + lax.div(t, 2) - 2 * lax.div(t, 3)
-        pair = lax.rem(lax.div(z, 2) + (2 * odd - 1) * turn + 8, 4)
-        slots = (choose(t, (0, 3, 4, 7), (1, 2, 5, 6)), choose(t, (2, 1, 6, 5), (0, 4, 3, 7)))
-
-        def keys_values(hi, carry):
-            for zl in range(2):
-                sorted_rows = jnp.dot(pick_v[...], slabs(hi, slots[zl]), preferred_element_type=F32).astype(BF16)
-                for p in range(4):
-                    W[hi, p, zl * 64 : zl * 64 + 64] = sorted_rows[p * 64 : p * 64 + 64]
-            kv = half_silu(0.5 * nt_dot(H[...].reshape(512, 1024), W[hi, 0:2].reshape(256, 1024)))
-            KV[t, hi, c, :, :128] = kv[:, :128].astype(BF16)
-            KV[t, hi, c, :, 128:] = (kv[:, 128:] * mask_v[...]).astype(BF16)
-            kv_copy(t, hi, c).start()
-            return carry
-
-        lax.fori_loop(0, 2, keys_values, 0)
-
-        def attend(hi, carry):
-            @pl.when((t == 0) & (hi == 0))
+        @pl.when(t < 4)
+        def _():
+            both(project, t)
+
+        @pl.when(t == 0)
+        def _():
+            third_second(2)
+            third_first(3)
+            third_first(4)
+
+        for w in (2, 3, 4):
+            @pl.when(t == w - 2)
             def _():
-                third_first(3)
-                third_first(4)
-
-            @pl.when((t == 0) & (hi == 1))
-            def _():
-                third_second(3)
-                third_second(4)
-
-            for w in (2, 3, 4):
-                @pl.when((t == w - 2) & (hi == 0))
-                def _():
-                    ring_wait(w)
-                    if w < 4:
-                        ring_send(w + 1)
-                    settle(plans[w][0][1] + plans[w][1][1])
-                    twin_send(w)
-
-            h = hi * 4 + pair
-            at = pl.ds(pl.multiple_of(h * 128, 128), 128)
-            for user in (c, oc):
-                if user is oc:
-                    kv_copy(t, hi, oc).wait_recv()
-                rows_c = cand_v[user]
-                qg = half_silu(0.5 * nt_dot(rows_c, W[hi, 2:4].reshape(256, 1024))).astype(BF16)
-                kv_c = half_silu(0.5 * nt_dot(rows_c, W[hi, 0:2].reshape(256, 1024))).astype(BF16)
-                queries = qg[:, :128]
-                gate[user, :, at] = qg[:, 128:]
-                keys, values = KV[t, hi, user, :, :128], KV[t, hi, user, :, 128:]
-                weights = half_silu(nt_dot(queries, keys) * score_half).astype(BF16)
-                att = jnp.dot(weights, values, preferred_element_type=F32)
-                own = jnp.sum(queries.astype(F32) * kv_c[:, :128].astype(F32), axis=1, keepdims=True)
-                own = half_silu(own * score_half)
-                attn[user, :, at] = att + own * kv_c[:, 128:].astype(F32)
-            return carry
-
-        lax.fori_loop(0, 2, attend, 0)
+                ring_wait(w)
+                if w < 4:
+                    ring_send(w + 1)
+                if w == 2:
+                    third_second(3)
+                if w == 3:
+                    third_second(4)
+                settle(plans[w][0][1] + plans[w][1][1])
+                twin_send(w)
+
+        @pl.when(t > 0)
+        def _():
+            both(attend, t - 1)
+
         return carry
 
     def kv_copy(t, hi, whose):
@@ -350,7 +373,7 @@
             send_sem=send_sem.at[k], recv_sem=recv_sem.at[k], device_id=sib, device_id_type=MESH,
         )
 
-    lax.fori_loop(0, HEADS // 2, chunk, 0)
+    lax.fori_loop(0, HEADS // 2 + 1, chunk, 0)
 
     slot0 = s * 384
 
@@ -400,7 +423,8 @@
             pltpu.VMEM((2, NX, NY, NZ, 16, 1024), BF16),
             pltpu.VMEM((NX, 2, 2, 32, 1024), BF16),
             pltpu.VMEM((4, 2, 2, 512, 256), BF16),
-            pltpu.VMEM((2, 4, 128, 1024), BF16),
+            pltpu.VMEM((2, 2, 2, 384, 128), BF16),
+            pltpu.VMEM((2, 2, 4, 128, 1024), BF16),
             pltpu.VMEM((256, 256), BF16),
             pltpu.VMEM((2, 384, 1024), BF16),
             pltpu.VMEM((1024, 1024), BF16),

time: 75.7 us -> 76.2 us (level)
  no operation moved by 1% of the time
where the time goes in v5:
time: 76.2 us; the launch traced here: 76.1 us
  Pallas kernels  73.4 us (96%)
  local copies, waits for them, and re-layouts  2.67 us (4%)
    pallas_call x1, Pallas kernels, body(): pl.pallas_call(kernel, out_shape=jax.ShapeDtypeStruct(candidates.shape, B...  73.4 us
    unnamed x1, local copies, waits for them, and re-layouts  2.67 us

profile of v5, /device:TPU:1, one launch (start us, length us, event | category | flops | bytes accessed | tf_op | source)
XLA Modules:
  0.0 76.1 jit_solution(796606219473245832)
XLA Ops:
  0.0 73.4 %shard_map.64 = bf16[2,384,1024]{2,1,0:T(8,128)(2,1)} custom-call(bf16[2,384,1024]{2,1,0:T(8,128)(2,1)} %cand_ref.1, bf16[2,32,1024]{2,1,0:T(8,128)(2,1)} %hist_ref.1, bf16[4,4,1024]{2,1,0:T(4,128)(2,1)} %proj_ref.1, bf16[1024,1024]{1,0:T(8,128)(2,1)} %ow_ref.1, s32[2]{0:T(128)} %hlen_ref.1, s32[2]{0:T(128)} %ccount_ref.1), custom_call_target="tpu_custom_call" | custom-call | tf_op jit(solution)/shard_map/pallas_call | solution.py:417
  73.4 2.7 %copy.8 = bf16[2,384,1024]{2,1,0:T(8,128)(2,1)} copy(bf16[2,384,1024]{2,1,0:T(8,128)(2,1)} %shard_map.64) | data formatting | bytes 3145728

commit v6 on v5

--- a/solution.py
+++ b/solution.py
@@ -120,18 +120,19 @@
         for where, k in arrivals:
             wait(where, k)
 
-    waves = [pl.ds(0, 1), pl.ds(1, 2), pl.ds(3, 2), pl.ds(5, 2), pl.ds(7, 1)]
+    waves = {2: pl.ds(3, 2), 3: pl.ds(5, 2), 4: pl.ds(7, 1)}
+    groups = [pl.ds(0, 3), pl.ds(3, 2), pl.ds(5, 3)]
 
     def second(w):
-        group_x = direct("y", lambda at: view(c, x, at, waves[w], COLS_X))
-        group_y = direct("x", lambda at: view(c, at, y, waves[w], COLS_Y))
+        group_x = direct("y", lambda at: view(c, x, at, groups[w], COLS_X))
+        group_y = direct("x", lambda at: view(c, at, y, groups[w], COLS_Y))
         return group_x, group_y
 
     def third(w, arrivals):
         settle(arrivals[0])
-        group_x = direct("x", lambda at: view(c, at, whole, waves[w], COLS_X))
+        group_x = direct("x", lambda at: view(c, at, whole, groups[w], COLS_X))
         settle(arrivals[1])
-        group_y = direct("y", lambda at: view(c, whole, at, waves[w], COLS_Y))
+        group_y = direct("y", lambda at: view(c, whole, at, groups[w], COLS_Y))
         return group_x + group_y
 
     spot = {"x": [up(x, NX, k) for k in range(NX)], "y": [up(y, NY, k) for k in range(NY)]}
@@ -158,12 +159,12 @@
         return whole if half is None else pl.ds(2 * half, 2)
 
     def wave_x(w):
-        return "x", lambda at, half: view(c, at, part(half), waves[w], COLS_X)
+        return "x", lambda at, half: view(c, at, part(half), groups[w], COLS_X)
 
     def wave_y(w):
-        return "y", lambda at, half: view(c, part(half), at, waves[w], COLS_Y)
-
-    plans = {w: (ring_plan(*wave_x(w)), ring_plan(*wave_y(w))) for w in (2, 3, 4)}
+        return "y", lambda at, half: view(c, part(half), at, groups[w], COLS_Y)
+
+    plans = {w: (ring_plan(*wave_x(w)), ring_plan(*wave_y(w))) for w in (1, 2)}
 
     def third_first(w):
         settle(stage2[w][0])
@@ -187,21 +188,20 @@
         along_z[SLOT[-off]] = (view(c, x, y, SLOT[-off], COLS_XY), k)
 
     zx = direct("x", lambda at: view(c, at, y, 0, COLS_Z))
-    z_send(1)
-    z_send(-1)
+    for off in (1, -1, 2, -2, 3, -3, 4):
+        z_send(off)
+    settle([along_z[1], along_z[2]])
     stage2 = {0: second(0)}
-    for off in (2, -2, 3, -3, 4):
-        z_send(off)
     settle(zx)
     zy = direct("y", lambda at: view(c, whole, at, 0, COLS_Z))
-    stage3 = {0: third(0, stage2[0])}
-    settle([along_z[1], along_z[2]])
+    settle([along_z[3], along_z[4]])
     stage2[1] = second(1)
     settle(zy)
 
     z_right, z_left = dev(x, y, up(z, NZ, 1), c), dev(x, y, up(z, NZ, -1), c)
     ring_sems = [(new_sem(), new_sem()) for _ in range(4)]
-    twin_sems = [new_sem() for _ in range(5)]
+    first_xy, first_z = new_sem(), new_sem()
+    twin_sems = {w: new_sem() for w in (2, 3, 4)}
     kv_sems = [new_sem() for _ in range(HEADS)]
 
     def ring_blocks(w):
@@ -229,27 +229,26 @@
         wait(view(oc, whole, whole, waves[w], whole), twin_sems[w])
 
     ring_send(1)
-    stage3[1] = third(1, stage2[1])
+    stage3 = third(0, stage2[0])
     local[0].wait()
     settle(hist_arrivals)
     ring_first("x", hist_block, hist_plan)
-    settle([along_z[3], along_z[4]])
+    settle([along_z[5], along_z[6], along_z[7]])
     stage2[2] = second(2)
-    settle(stage3[0])
-    twin_send(0)
-    settle([along_z[5], along_z[6], along_z[7]])
-    stage2[3] = second(3)
-    stage2[4] = second(4)
     ring_wait(1)
     ring_send(2)
-    settle(stage3[1])
-    twin_send(1)
+    block = view(c, whole, whole, groups[0], COLS_Z)
+    send(block, block, first_z, sib)
+    third_first(1)
+    settle(stage3)
+    block_xy = view(c, whole, whole, groups[0], COLS_XY)
+    send(block_xy, block_xy, first_xy, sib)
+    ring_second("x", hist_block, hist_plan)
     third_first(2)
-    ring_second("x", hist_block, hist_plan)
     local[1].wait()
     local[2].wait()
-    twin_wait(0)
-    twin_wait(1)
+    wait(view(oc, whole, whole, groups[0], COLS_Z), first_z)
+    wait(view(oc, whole, whole, groups[0], COLS_XY), first_xy)
 
     head_size = 128
     score_half = 0.5 / math.sqrt(head_size)
@@ -291,15 +290,16 @@
             sorted_rows = jnp.dot(pick_v[...], slabs(hi, slots[zl]), preferred_element_type=F32).astype(BF16)
             for p in range(4):
                 W[keep, hi, p, zl * 64 : zl * 64 + 64] = sorted_rows[p * 64 : p * 64 + 64]
+        parts = half_silu(0.5 * nt_dot(cand_v[...].reshape(768, 1024), W[keep, hi].reshape(512, 1024))).astype(BF16)
+        own_keys, own_values = parts[:, :128], parts[:, 128:256]
+        queries, user_gate = parts[:, 256:384], parts[:, 384:]
+        own = jnp.dot(queries * own_keys, jnp.ones((128, 128), BF16), preferred_element_type=F32)
+        own = half_silu(own * score_half) * own_values.astype(F32)
         for user in range(users_here):
-            rows_c = cand_v[user]
-            qg = half_silu(0.5 * nt_dot(rows_c, W[keep, hi, 2:4].reshape(256, 1024))).astype(BF16)
-            kv_c = half_silu(0.5 * nt_dot(rows_c, W[keep, hi, 0:2].reshape(256, 1024))).astype(BF16)
-            queries = qg[:, :128]
-            Q[keep, hi, user] = queries
-            gate[user, :, at] = qg[:, 128:]
-            own = jnp.sum(queries.astype(F32) * kv_c[:, :128].astype(F32), axis=1, keepdims=True)
-            attn[user, :, at] = half_silu(own * score_half) * kv_c[:, 128:].astype(F32)
+            rows_u = slice(user * 384, user * 384 + 384)
+            Q[keep, hi, user] = queries[rows_u]
+            gate[user, :, at] = user_gate[rows_u]
+            attn[user, :, at] = own[rows_u]
 
     def keys_values(t, hi):
         w_kv = W[lax.rem(t, 2), hi, 0:2].reshape(256, 1024)
@@ -341,28 +341,35 @@
         def _():
             both(project, t)
 
+        def forward(w):
+            ring_wait(w)
+            if w < 4:
+                ring_send(w + 1)
+            if w == 2:
+                third_second(1)
+                settle(plans[1][0][1] + plans[1][1][1])
+            if w == 3:
+                settle(plans[2][0][1] + plans[2][1][1])
+            twin_send(w)
+            if w == 2:
+                third_second(2)
+
         @pl.when(t == 0)
         def _():
-            third_second(2)
-            third_first(3)
-            third_first(4)
-
-        for w in (2, 3, 4):
+            forward(2)
+
+        @pl.when(t > 0)
+        def _():
+            attend(t - 1, 0)
+
+        for w in (3, 4):
             @pl.when(t == w - 2)
             def _():
-                ring_wait(w)
-                if w < 4:
-                    ring_send(w + 1)
-                if w == 2:
-                    third_second(3)
-                if w == 3:
-                    third_second(4)
-                settle(plans[w][0][1] + plans[w][1][1])
-                twin_send(w)
+                forward(w)
 
         @pl.when(t > 0)
         def _():
-            both(attend, t - 1)
+            attend(t - 1, 1)
 
         return carry
 

time: 76.2 us -> 74.5 us (0.978)
  Pallas kernels: 73.4 us -> 71.7 us
    pallas_call x1, Pallas kernels: 73.4 us -> 71.7 us  [body(): pl.pallas_call(kernel, out_shape=jax.ShapeDtypeStruct(candidates.shape, B...]
where the time goes in v6:
time: 74.5 us; the launch traced here: 74.4 us
  Pallas kernels  71.7 us (96%)
  local copies, waits for them, and re-layouts  2.67 us (4%)
    pallas_call x1, Pallas kernels, body(): pl.pallas_call(kernel, out_shape=jax.ShapeDtypeStruct(candidates.shape, B...  71.7 us
    unnamed x1, local copies, waits for them, and re-layouts  2.67 us

profile of v6, /device:TPU:1, one launch (start us, length us, event | category | flops | bytes accessed | tf_op | source)
XLA Modules:
  0.0 74.4 jit_solution(235069563257019090)
XLA Ops:
  0.0 71.7 %shard_map.64 = bf16[2,384,1024]{2,1,0:T(8,128)(2,1)} custom-call(bf16[2,384,1024]{2,1,0:T(8,128)(2,1)} %cand_ref.1, bf16[2,32,1024]{2,1,0:T(8,128)(2,1)} %hist_ref.1, bf16[4,4,1024]{2,1,0:T(4,128)(2,1)} %proj_ref.1, bf16[1024,1024]{1,0:T(8,128)(2,1)} %ow_ref.1, s32[2]{0:T(128)} %hlen_ref.1, s32[2]{0:T(128)} %ccount_ref.1), custom_call_target="tpu_custom_call" | custom-call | tf_op jit(solution)/shard_map/pallas_call | solution.py:424
  71.7 2.7 %copy.8 = bf16[2,384,1024]{2,1,0:T(8,128)(2,1)} copy(bf16[2,384,1024]{2,1,0:T(8,128)(2,1)} %shard_map.64) | data formatting | bytes 3145728

commit v7 on v6

--- a/solution.py
+++ b/solution.py
@@ -155,27 +155,6 @@
             mine = block(spot[axis][4 - step], half)
             send(mine, mine, plan[1][half][1], neighbour[axis][step])
 
-    def part(half):
-        return whole if half is None else pl.ds(2 * half, 2)
-
-    def wave_x(w):
-        return "x", lambda at, half: view(c, at, part(half), groups[w], COLS_X)
-
-    def wave_y(w):
-        return "y", lambda at, half: view(c, part(half), at, groups[w], COLS_Y)
-
-    plans = {w: (ring_plan(*wave_x(w)), ring_plan(*wave_y(w))) for w in (1, 2)}
-
-    def third_first(w):
-        settle(stage2[w][0])
-        ring_first(*wave_x(w), plans[w][0])
-        settle(stage2[w][1])
-        ring_first(*wave_y(w), plans[w][1])
-
-    def third_second(w):
-        ring_second(*wave_x(w), plans[w][0])
-        ring_second(*wave_y(w), plans[w][1])
-
     def hist_block(at, half):
         return (lambda: H.at[at]) if half is None else (lambda: H.at[at, half])
 
@@ -239,12 +218,12 @@
     ring_send(2)
     block = view(c, whole, whole, groups[0], COLS_Z)
     send(block, block, first_z, sib)
-    third_first(1)
+    later = {1: third(1, stage2[1])}
     settle(stage3)
     block_xy = view(c, whole, whole, groups[0], COLS_XY)
     send(block_xy, block_xy, first_xy, sib)
     ring_second("x", hist_block, hist_plan)
-    third_first(2)
+    later[2] = third(2, stage2[2])
     local[1].wait()
     local[2].wait()
     wait(view(oc, whole, whole, groups[0], COLS_Z), first_z)
@@ -331,6 +310,7 @@
         @pl.when(t > 0)
         def _():
             both(keys_values, t - 1)
+            both(attend, t - 1)
 
         for w in (2, 3, 4):
             @pl.when(t == w - 1)
@@ -345,31 +325,14 @@
             ring_wait(w)
             if w < 4:
                 ring_send(w + 1)
-            if w == 2:
-                third_second(1)
-                settle(plans[1][0][1] + plans[1][1][1])
-            if w == 3:
-                settle(plans[2][0][1] + plans[2][1][1])
+            if w < 4:
+                settle(later[w - 1])
             twin_send(w)
-            if w == 2:
-                third_second(2)
-
-        @pl.when(t == 0)
-        def _():
-            forward(2)
-
-        @pl.when(t > 0)
-        def _():
-            attend(t - 1, 0)
-
-        for w in (3, 4):
+
+        for w in (2, 3, 4):
             @pl.when(t == w - 2)
             def _():
                 forward(w)
-
-        @pl.when(t > 0)
-        def _():
-            attend(t - 1, 1)
 
         return carry
 

time: 74.5 us -> 73.3 us (0.984)
  Pallas kernels: 71.7 us -> 70.5 us
    pallas_call x1, Pallas kernels: 71.7 us -> 70.5 us  [body(): pl.pallas_call(kernel, out_shape=jax.ShapeDtypeStruct(candidates.shape, B...]
where the time goes in v7:
time: 73.3 us; the launch traced here: 73.1 us
  Pallas kernels  70.5 us (96%)
  local copies, waits for them, and re-layouts  2.67 us (4%)
    pallas_call x1, Pallas kernels, body(): pl.pallas_call(kernel, out_shape=jax.ShapeDtypeStruct(candidates.shape, B...  70.5 us
    unnamed x1, local copies, waits for them, and re-layouts  2.67 us

profile of v7, /device:TPU:1, one launch (start us, length us, event | category | flops | bytes accessed | tf_op | source)
XLA Modules:
  0.0 73.1 jit_solution(2164269013787081347)
XLA Ops:
  0.0 70.5 %shard_map.64 = bf16[2,384,1024]{2,1,0:T(8,128)(2,1)} custom-call(bf16[2,384,1024]{2,1,0:T(8,128)(2,1)} %cand_ref.1, bf16[2,32,1024]{2,1,0:T(8,128)(2,1)} %hist_ref.1, bf16[4,4,1024]{2,1,0:T(4,128)(2,1)} %proj_ref.1, bf16[1024,1024]{1,0:T(8,128)(2,1)} %ow_ref.1, s32[2]{0:T(128)} %hlen_ref.1, s32[2]{0:T(128)} %ccount_ref.1), custom_call_target="tpu_custom_call" | custom-call | tf_op jit(solution)/shard_map/pallas_call | solution.py:387
  70.5 2.7 %copy.8 = bf16[2,384,1024]{2,1,0:T(8,128)(2,1)} copy(bf16[2,384,1024]{2,1,0:T(8,128)(2,1)} %shard_map.64) | data formatting | bytes 3145728

commit v8 on v7

--- a/solution.py
+++ b/solution.py
@@ -287,20 +287,15 @@
         KV[t, hi, c, :, 128:] = (kv[:, 128:] * mask_v[...]).astype(BF16)
         kv_copy(t, hi, c).start()
 
-    def attend(t, hi):
-        kv_copy(t, hi, oc).wait_recv()
+    def attend(t, hi, user):
         keep, at = lax.rem(t, 2), columns_of(t, hi)
-        for user in range(users_here):
-            keys, values = KV[t, hi, user, :, :128], KV[t, hi, user, :, 128:]
-            weights = half_silu(nt_dot(Q[keep, hi, user], keys) * score_half).astype(BF16)
-            attn[user, :, at] += jnp.dot(weights, values, preferred_element_type=F32)
+        keys, values = KV[t, hi, user, :, :128], KV[t, hi, user, :, 128:]
+        weights = half_silu(nt_dot(Q[keep, hi, user], keys) * score_half).astype(BF16)
+        attn[user, :, at] += jnp.dot(weights, values, preferred_element_type=F32)
 
     def both(work, t):
-        def step(hi, carry):
+        for hi in range(2):
             work(t, hi)
-            return carry
-
-        lax.fori_loop(0, 2, step, 0)
 
     def chunk(t, carry):
         @pl.when(t == 1)
@@ -310,7 +305,10 @@
         @pl.when(t > 0)
         def _():
             both(keys_values, t - 1)
-            both(attend, t - 1)
+            both(functools.partial(attend, user=c), t - 1)
+            for hi in range(2):
+                kv_copy(t - 1, hi, oc).wait_recv()
+            both(functools.partial(attend, user=oc), t - 1)
 
         for w in (2, 3, 4):
             @pl.when(t == w - 1)

time: 73.3 us -> 73 us (level)
  no operation moved by 1% of the time
where the time goes in v8:
time: 73 us; the launch traced here: 72.8 us
  Pallas kernels  70.2 us (96%)
  local copies, waits for them, and re-layouts  2.67 us (4%)
    pallas_call x1, Pallas kernels, body(): pl.pallas_call(kernel, out_shape=jax.ShapeDtypeStruct(candidates.shape, B...  70.2 us
    unnamed x1, local copies, waits for them, and re-layouts  2.67 us

profile of v8, /device:TPU:1, one launch (start us, length us, event | category | flops | bytes accessed | tf_op | source)
XLA Modules:
  0.0 72.8 jit_solution(8054276115898435329)
XLA Ops:
  0.0 70.2 %shard_map.64 = bf16[2,384,1024]{2,1,0:T(8,128)(2,1)} custom-call(bf16[2,384,1024]{2,1,0:T(8,128)(2,1)} %cand_ref.1, bf16[2,32,1024]{2,1,0:T(8,128)(2,1)} %hist_ref.1, bf16[4,4,1024]{2,1,0:T(4,128)(2,1)} %proj_ref.1, bf16[1024,1024]{1,0:T(8,128)(2,1)} %ow_ref.1, s32[2]{0:T(128)} %hlen_ref.1, s32[2]{0:T(128)} %ccount_ref.1), custom_call_target="tpu_custom_call" | custom-call | tf_op jit(solution)/shard_map/pallas_call | solution.py:385
  70.2 2.7 %copy.8 = bf16[2,384,1024]{2,1,0:T(8,128)(2,1)} copy(bf16[2,384,1024]{2,1,0:T(8,128)(2,1)} %shard_map.64) | data formatting | bytes 3145728

commit v9 on v8

--- a/solution.py
+++ b/solution.py
@@ -135,30 +135,6 @@
         group_y = direct("y", lambda at: view(c, whole, at, groups[w], COLS_Y))
         return group_x + group_y
 
-    spot = {"x": [up(x, NX, k) for k in range(NX)], "y": [up(y, NY, k) for k in range(NY)]}
-    neighbour = {
-        "x": [dev(spot["x"][k], y, z, c) for k in range(NX)],
-        "y": [dev(x, spot["y"][k], z, c) for k in range(NY)],
-    }
-
-    def ring_plan(axis, block):
-        first = [(block(spot[axis][3], None), new_sem()), (block(spot[axis][1], None), new_sem())]
-        return first, [(block(spot[axis][2], half), new_sem()) for half in range(2)]
-
-    def ring_first(axis, block, plan):
-        for (_, k), step in zip(plan[0], (1, 3)):
-            send(block(spot[axis][0], None), block(spot[axis][0], None), k, neighbour[axis][step])
-
-    def ring_second(axis, block, plan):
-        settle(plan[0])
-        for half, step in ((0, 1), (1, 3)):
-            mine = block(spot[axis][4 - step], half)
-            send(mine, mine, plan[1][half][1], neighbour[axis][step])
-
-    def hist_block(at, half):
-        return (lambda: H.at[at]) if half is None else (lambda: H.at[at, half])
-
-    hist_plan = ring_plan("x", hist_block)
     along_z = {}
 
     def z_send(off):
@@ -211,7 +187,7 @@
     stage3 = third(0, stage2[0])
     local[0].wait()
     settle(hist_arrivals)
-    ring_first("x", hist_block, hist_plan)
+    hist_x = direct("x", lambda at: lambda: H.at[at])
     settle([along_z[5], along_z[6], along_z[7]])
     stage2[2] = second(2)
     ring_wait(1)
@@ -222,12 +198,11 @@
     settle(stage3)
     block_xy = view(c, whole, whole, groups[0], COLS_XY)
     send(block_xy, block_xy, first_xy, sib)
-    ring_second("x", hist_block, hist_plan)
-    later[2] = third(2, stage2[2])
     local[1].wait()
     local[2].wait()
     wait(view(oc, whole, whole, groups[0], COLS_Z), first_z)
     wait(view(oc, whole, whole, groups[0], COLS_XY), first_xy)
+    later[2] = third(2, stage2[2])
 
     head_size = 128
     score_half = 0.5 / math.sqrt(head_size)
@@ -300,7 +275,7 @@
     def chunk(t, carry):
         @pl.when(t == 1)
         def _():
-            settle(hist_plan[1])
+            settle(hist_x)
 
         @pl.when(t > 0)
         def _():

time: 73 us -> 77.4 us (1.060)
  Pallas kernels: 70.2 us -> 74.5 us
    pallas_call x1, Pallas kernels: 70.2 us -> 74.5 us  [body(): pl.pallas_call(kernel, out_shape=jax.ShapeDtypeStruct(candidates.shape, B...]
where the time goes in v9:
time: 77.4 us; the launch traced here: 77.2 us
  Pallas kernels  74.5 us (96%)
  local copies, waits for them, and re-layouts  2.67 us (3%)
    pallas_call x1, Pallas kernels, body(): pl.pallas_call(kernel, out_shape=jax.ShapeDtypeStruct(candidates.shape, B...  74.5 us
    unnamed x1, local copies, waits for them, and re-layouts  2.67 us

profile of v9, /device:TPU:1, one launch (start us, length us, event | category | flops | bytes accessed | tf_op | source)
XLA Modules:
  0.0 77.2 jit_solution(3186211394188289586)
XLA Ops:
  0.0 74.5 %shard_map.64 = bf16[2,384,1024]{2,1,0:T(8,128)(2,1)} custom-call(bf16[2,384,1024]{2,1,0:T(8,128)(2,1)} %cand_ref.1, bf16[2,32,1024]{2,1,0:T(8,128)(2,1)} %hist_ref.1, bf16[4,4,1024]{2,1,0:T(4,128)(2,1)} %proj_ref.1, bf16[1024,1024]{1,0:T(8,128)(2,1)} %ow_ref.1, s32[2]{0:T(128)} %hlen_ref.1, s32[2]{0:T(128)} %ccount_ref.1), custom_call_target="tpu_custom_call" | custom-call | tf_op jit(solution)/shard_map/pallas_call | solution.py:360
  74.5 2.7 %copy.8 = bf16[2,384,1024]{2,1,0:T(8,128)(2,1)} copy(bf16[2,384,1024]{2,1,0:T(8,128)(2,1)} %shard_map.64) | data formatting | bytes 3145728

commit v10 on v8

--- a/solution.py
+++ b/solution.py
@@ -171,6 +171,9 @@
         z_send(off)
     settle([along_z[1], along_z[2]])
     stage2 = {0: second(0)}
+    local[0].wait()
+    settle(hist_arrivals)
+    ring_first("x", hist_block, hist_plan)
     settle(zx)
     zy = direct("y", lambda at: view(c, whole, at, 0, COLS_Z))
     settle([along_z[3], along_z[4]])
@@ -209,9 +212,6 @@
 
     ring_send(1)
     stage3 = third(0, stage2[0])
-    local[0].wait()
-    settle(hist_arrivals)
-    ring_first("x", hist_block, hist_plan)
     settle([along_z[5], along_z[6], along_z[7]])
     stage2[2] = second(2)
     ring_wait(1)

time: 73 us -> 69.4 us (0.951)
  Pallas kernels: 70.2 us -> 66.5 us
    pallas_call x1, Pallas kernels: 70.2 us -> 66.5 us  [body(): pl.pallas_call(kernel, out_shape=jax.ShapeDtypeStruct(candidates.shape, B...]
where the time goes in v10:
time: 69.4 us; the launch traced here: 69.2 us
  Pallas kernels  66.5 us (96%)
  local copies, waits for them, and re-layouts  2.67 us (4%)
    pallas_call x1, Pallas kernels, body(): pl.pallas_call(kernel, out_shape=jax.ShapeDtypeStruct(candidates.shape, B...  66.5 us
    unnamed x1, local copies, waits for them, and re-layouts  2.67 us

profile of v10, /device:TPU:1, one launch (start us, length us, event | category | flops | bytes accessed | tf_op | source)
XLA Modules:
  0.0 69.2 jit_solution(16690291651854966973)
XLA Ops:
  0.0 66.5 %shard_map.64 = bf16[2,384,1024]{2,1,0:T(8,128)(2,1)} custom-call(bf16[2,384,1024]{2,1,0:T(8,128)(2,1)} %cand_ref.1, bf16[2,32,1024]{2,1,0:T(8,128)(2,1)} %hist_ref.1, bf16[4,4,1024]{2,1,0:T(4,128)(2,1)} %proj_ref.1, bf16[1024,1024]{1,0:T(8,128)(2,1)} %ow_ref.1, s32[2]{0:T(128)} %hlen_ref.1, s32[2]{0:T(128)} %ccount_ref.1), custom_call_target="tpu_custom_call" | custom-call | tf_op jit(solution)/shard_map/pallas_call | solution.py:385
  66.5 2.7 %copy.8 = bf16[2,384,1024]{2,1,0:T(8,128)(2,1)} copy(bf16[2,384,1024]{2,1,0:T(8,128)(2,1)} %shard_map.64) | data formatting | bytes 3145728

commit v11 on v10

--- a/solution.py
+++ b/solution.py
@@ -218,11 +218,11 @@
     ring_send(2)
     block = view(c, whole, whole, groups[0], COLS_Z)
     send(block, block, first_z, sib)
+    ring_second("x", hist_block, hist_plan)
     later = {1: third(1, stage2[1])}
     settle(stage3)
     block_xy = view(c, whole, whole, groups[0], COLS_XY)
     send(block_xy, block_xy, first_xy, sib)
-    ring_second("x", hist_block, hist_plan)
     later[2] = third(2, stage2[2])
     local[1].wait()
     local[2].wait()

time: 69.4 us -> 70.1 us (1.010)
  Pallas kernels: 66.5 us -> 67.3 us
    pallas_call x1, Pallas kernels: 66.5 us -> 67.3 us  [body(): pl.pallas_call(kernel, out_shape=jax.ShapeDtypeStruct(candidates.shape, B...]
where the time goes in v11:
time: 70.1 us; the launch traced here: 69.9 us
  Pallas kernels  67.3 us (96%)
  local copies, waits for them, and re-layouts  2.67 us (4%)
    pallas_call x1, Pallas kernels, body(): pl.pallas_call(kernel, out_shape=jax.ShapeDtypeStruct(candidates.shape, B...  67.3 us
    unnamed x1, local copies, waits for them, and re-layouts  2.67 us

profile of v11, /device:TPU:1, one launch (start us, length us, event | category | flops | bytes accessed | tf_op | source)
XLA Modules:
  0.0 69.9 jit_solution(9684607742697422028)
XLA Ops:
  0.0 67.3 %shard_map.64 = bf16[2,384,1024]{2,1,0:T(8,128)(2,1)} custom-call(bf16[2,384,1024]{2,1,0:T(8,128)(2,1)} %cand_ref.1, bf16[2,32,1024]{2,1,0:T(8,128)(2,1)} %hist_ref.1, bf16[4,4,1024]{2,1,0:T(4,128)(2,1)} %proj_ref.1, bf16[1024,1024]{1,0:T(8,128)(2,1)} %ow_ref.1, s32[2]{0:T(128)} %hlen_ref.1, s32[2]{0:T(128)} %ccount_ref.1), custom_call_target="tpu_custom_call" | custom-call | tf_op jit(solution)/shard_map/pallas_call | solution.py:385
  67.3 2.7 %copy.8 = bf16[2,384,1024]{2,1,0:T(8,128)(2,1)} copy(bf16[2,384,1024]{2,1,0:T(8,128)(2,1)} %shard_map.64) | data formatting | bytes 3145728
